TPU v7x, 768 devices: a whole 4x8x12 slice. The times are simulated.
768 devices in a mesh: panel: 2 (over y_lo), lat: 12 (over z), lon: 32 (over y_hi, x, core).
Axes of the slice: x: 4, y: 8 (y_hi: 4, y_lo: 2; y = y_hi * 2 + y_lo), z: 12, core: 2. Of those that a mesh axis runs over, the one named last changes fastest.
Arguments:
- field: float32 [2, 3, 2, 1536, 4096], P('panel', None, None, 'lat', 'lon'), may hold values from -6 to 6
- velocity: float32 [2, 2, 2, 1536, 4096], P('panel', None, None, 'lat', 'lon'), may hold values from -0.5 to 0.5
- diffusion: float32 [3], replicated, may hold values from 0.02 to 0.08
- donor_cell: int32 [2, 12, 32, 118], P('panel', 'lat', 'lon'), may hold values from 0 to 15996, as said below
- donor_weight: float32 [2, 12, 32, 16, 118], P('panel', 'lat', 'lon'), as said below
- source_tile: int32 [2, 12, 32, 508], P('panel', 'lat', 'lon'), may hold values from 0 to 383, as said below
- source_slot: int32 [2, 12, 32, 508], P('panel', 'lat', 'lon'), may hold values from 0 to 117
- recv_cell: int32 [2, 12, 32, 508], P('panel', 'lat', 'lon'), may hold values from 0 to 16383, as said below
Outputs:
- stepped: float32 [2, 3, 2, 1536, 4096], P('panel', None, None, 'lat', 'lon')
Inputs may be any that keep to these rules, and one draw needn't show every extreme that they name: `donor_cell`: the block lies inside the tile: its row is at most 124 and its column at most 124. `donor_weight`: bicubic Lagrange weights of a point inside the block's middle cell, row-major over the block; each slot's weights sum to one. `source_tile`: no two live rows of one panel name the same donor tile and slot. `recv_cell`: the live rows of a tile name its receptor cells, each once.
All inputs are finite; a program needn't handle non-finite values.
Results may differ from a plain program's by a relative error of at most 0.0003.
Values sent between devices are 32-bit elements; how exact they have to be, the bound alone decides.
No kernel may reach another device: no remote copies, remote signals or barrier semaphores. Data moves between devices by JAX's collectives and lax.ppermute only.
A program may use at most 128 MiB of HBM per device.

v0:
```python
import jax
import jax.numpy as jnp
from jax import lax
from jax.sharding import PartitionSpec as P


def with_halo(array, sides, width):
    for axis, dim in sides:
        size, length = (lax.axis_size(axis), array.shape[dim])
        up = [(i, (i + 1) % size) for i in range(size - 1)]
        down = [(j, i) for i, j in up]
        last = lax.slice_in_dim(array, length - width, length, axis=dim)
        first = lax.slice_in_dim(array, 0, width, axis=dim)
        before = lax.ppermute(last, axis, up)
        after = lax.ppermute(first, axis, down)
        array = jnp.concatenate([before, array, after], axis=dim)
    return array


def from_partner(block, axis, stride):
    count = lax.axis_size(axis)
    route = []
    for low in range(count):
        high = low | 1 << stride
        if high != low and high < count:
            route += [(low, high), (high, low)]
    return lax.ppermute(block, axis, route)


def advance(padded, state, velocity, diffusion):
    height = state.shape[2]
    breadth = state.shape[3]

    def along_th(offset):
        return padded[:, :, 2 + offset : 2 + offset + height, 2 : 2 + breadth]

    def along_ph(offset):
        return padded[:, :, 2 : 2 + height, 2 + offset : 2 + offset + breadth]

    slope_th = (along_th(-2) - along_th(2) + 8.0 * (along_th(1) - along_th(-1))) / 12.0
    curve_th = (
        16.0 * (along_th(1) + along_th(-1)) - along_th(2) - along_th(-2) - 30.0 * state
    ) / 12.0
    slope_ph = (along_ph(-2) - along_ph(2) + 8.0 * (along_ph(1) - along_ph(-1))) / 12.0
    curve_ph = (
        16.0 * (along_ph(1) + along_ph(-1)) - along_ph(2) - along_ph(-2) - 30.0 * state
    ) / 12.0
    carried = velocity[0][None] * slope_th + velocity[1][None] * slope_ph
    return state - carried + diffusion[:, None, None, None] * (curve_th + curve_ph)


def interpolate(flattened, corners, weights, breadth):
    summed = jnp.zeros((flattened.shape[0], corners.shape[0]), jnp.float32)
    for vertical in range(4):
        for lateral in range(4):
            picked = jnp.take(flattened, corners + vertical * breadth + lateral, axis=1)
            summed = summed + weights[vertical * 4 + lateral][None, :] * picked
    return summed


def pick_rows(piece, donor_tiles, donor_slots):
    piece_count = piece.shape[1]
    slot_count = piece.shape[2]
    inside = (donor_tiles >= 0) & (donor_tiles < piece_count)
    column_index = jnp.clip(donor_tiles, 0, piece_count - 1) * slot_count + donor_slots
    flattened_piece = piece.reshape(piece.shape[0], piece_count * slot_count)
    picked = jnp.take(flattened_piece, column_index, axis=1)
    return jnp.where(inside[None, :], picked, 0.0)


def per_device(
    field, velocity, diffusion, donor_cell, donor_weight, source_tile, source_slot, recv_cell
):
    state = field[0]
    field_count, radius_count, height, breadth = state.shape
    channels = field_count * radius_count
    lat_count = lax.axis_size("lat")
    lon_count = lax.axis_size("lon")
    rows_cap = recv_cell.shape[-1]
    flattened = state.reshape(channels, height * breadth)
    donated = interpolate(flattened, donor_cell[0, 0, 0], donor_weight[0, 0, 0], breadth)[
        :, None, :
    ]
    row_index = lax.axis_index("lat") * height + jnp.arange(height)
    col_index = lax.axis_index("lon") * breadth + jnp.arange(breadth)
    edge_rows = (row_index < 2) | (row_index >= height * lat_count - 2)
    edge_cols = (col_index < 2) | (col_index >= breadth * lon_count - 2)
    edge_band = edge_rows[:, None] | edge_cols[None, :]
    edge_count = jnp.sum(edge_band.astype(jnp.int32))
    live_rows = (jnp.arange(rows_cap) < edge_count).astype(jnp.float32)
    padded = with_halo(field, (("lat", 3), ("lon", 4)), 2)
    advanced = advance(padded[0], state, velocity[0], diffusion).reshape(channels, height * breadth)
    crossed = from_partner(donated, "panel", 0)
    own_tiles = source_tile[0, 0, 0]
    own_slots = source_slot[0, 0, 0]
    picked = pick_rows(
        lax.all_gather(crossed, ("lat", "lon"), axis=1, tiled=True), own_tiles, own_slots
    )
    picked = picked * live_rows[None, :]
    receptor_cells = recv_cell[0, 0, 0]
    landed = jnp.zeros((channels, height * breadth), jnp.float32).at[:, receptor_cells].add(picked)
    presence = jnp.zeros((height * breadth,), jnp.float32).at[receptor_cells].add(live_rows)
    result = jnp.where(presence[None, :] > 0.5, landed, advanced)
    return result.reshape(1, field_count, radius_count, height, breadth)


def solution(mesh):
    placed = (
        P("panel", None, None, "lat", "lon"),
        P("panel", None, None, "lat", "lon"),
        P(),
        P("panel", "lat", "lon", None),
        P("panel", "lat", "lon", None, None),
        P("panel", "lat", "lon", None),
        P("panel", "lat", "lon", None),
        P("panel", "lat", "lon", None),
    )
    return jax.shard_map(
        per_device,
        mesh=mesh,
        in_specs=placed,
        out_specs=P("panel", None, None, "lat", "lon"),
        check_vma=False,
    )
```

profile of v0, /device:TPU:1, one launch (start us, length us, event | category | flops | bytes accessed | tf_op | source)
XLA Modules:
  0.0 307.4 jit_solution(6375023333390143851)
XLA Ops:
  8.1 1.2 copy.116
  9.4 5.3 %copy.74 = f32[6,16384]{0,1:T(8,128)} copy(f32[6,16384]{1,0:T(8,128)S(1)} %bitcast.243) | data formatting | bytes 786432 | tf_op jit(solution)/shard_map/reshape;squeeze | solution.py:80
  14.7 4.0 %gather_fusion.13 = f32[118,6]{1,0:T(8,128)S(1)} fusion(f32[6,16384]{0,1:T(8,128)} %copy.74, s32[1024]{0:T(1024)S(1)} %get-tuple-element.94), kind=kCustom, calls=%fused_computation.13.clone | custom fusion | bytes 6136 | tf_op jit(solution)/shard_map/jit(_take)/gather | solution.py:56
  18.8 4.0 %gather_fusion.14 = f32[118,6]{1,0:T(8,128)S(1)} fusion(f32[6,16384]{0,1:T(8,128)} %copy.74, s32[1024]{0:T(1024)S(1)} %get-tuple-element.93), kind=kCustom, calls=%fused_computation.14.clone | custom fusion | bytes 6136 | tf_op jit(solution)/shard_map/jit(_take)/gather | solution.py:56
  22.9 4.0 %gather_fusion.2 = f32[118,6]{1,0:T(8,128)S(1)} fusion(f32[6,16384]{0,1:T(8,128)} %copy.74, s32[1024]{0:T(1024)S(1)} %get-tuple-element.105), kind=kCustom, calls=%fused_computation.2.clone | custom fusion | bytes 6136 | tf_op jit(solution)/shard_map/jit(_take)/gather | solution.py:56
  27.0 4.0 %gather_fusion.3 = f32[118,6]{1,0:T(8,128)S(1)} fusion(f32[6,16384]{0,1:T(8,128)} %copy.74, s32[1024]{0:T(1024)S(1)} %get-tuple-element.104), kind=kCustom, calls=%fused_computation.3.clone | custom fusion | bytes 6136 | tf_op jit(solution)/shard_map/jit(_take)/gather | solution.py:56
  31.1 4.0 %gather_fusion.4 = f32[118,6]{1,0:T(8,128)S(1)} fusion(f32[6,16384]{0,1:T(8,128)} %copy.74, s32[1024]{0:T(1024)S(1)} %get-tuple-element.103), kind=kCustom, calls=%fused_computation.4.clone | custom fusion | bytes 6136 | tf_op jit(solution)/shard_map/jit(_take)/gather | solution.py:56
  35.2 4.0 %gather_fusion.5 = f32[118,6]{1,0:T(8,128)S(1)} fusion(f32[6,16384]{0,1:T(8,128)} %copy.74, s32[1024]{0:T(1024)S(1)} %get-tuple-element.102), kind=kCustom, calls=%fused_computation.5.clone | custom fusion | bytes 6136 | tf_op jit(solution)/shard_map/jit(_take)/gather | solution.py:56
  39.3 4.0 %gather_fusion.6 = f32[118,6]{1,0:T(8,128)S(1)} fusion(f32[6,16384]{0,1:T(8,128)} %copy.74, s32[1024]{0:T(1024)S(1)} %get-tuple-element.101), kind=kCustom, calls=%fused_computation.6.clone | custom fusion | bytes 6136 | tf_op jit(solution)/shard_map/jit(_take)/gather | solution.py:56
  43.4 4.0 %gather_fusion.7 = f32[118,6]{1,0:T(8,128)S(1)} fusion(f32[6,16384]{0,1:T(8,128)} %copy.74, s32[1024]{0:T(1024)S(1)} %get-tuple-element.100), kind=kCustom, calls=%fused_computation.7.clone | custom fusion | bytes 6136 | tf_op jit(solution)/shard_map/jit(_take)/gather | solution.py:56
  47.5 4.0 %gather_fusion.8 = f32[118,6]{1,0:T(8,128)S(1)} fusion(f32[6,16384]{0,1:T(8,128)} %copy.74, s32[1024]{0:T(1024)S(1)} %get-tuple-element.99), kind=kCustom, calls=%fused_computation.8.clone | custom fusion | bytes 6136 | tf_op jit(solution)/shard_map/jit(_take)/gather | solution.py:56
  51.6 4.0 %gather_fusion.9 = f32[118,6]{1,0:T(8,128)S(1)} fusion(f32[6,16384]{0,1:T(8,128)} %copy.74, s32[1024]{0:T(1024)S(1)} %get-tuple-element.98), kind=kCustom, calls=%fused_computation.9.clone | custom fusion | bytes 6136 | tf_op jit(solution)/shard_map/jit(_take)/gather | solution.py:56
  55.8 4.0 %gather_fusion.10 = f32[118,6]{1,0:T(8,128)S(1)} fusion(f32[6,16384]{0,1:T(8,128)} %copy.74, s32[1024]{0:T(1024)S(1)} %get-tuple-element.97), kind=kCustom, calls=%fused_computation.10.clone | custom fusion | bytes 6136 | tf_op jit(solution)/shard_map/jit(_take)/gather | solution.py:56
  59.9 4.0 %gather_fusion.11 = f32[118,6]{1,0:T(8,128)S(1)} fusion(f32[6,16384]{0,1:T(8,128)} %copy.74, s32[1024]{0:T(1024)S(1)} %get-tuple-element.96), kind=kCustom, calls=%fused_computation.11.clone | custom fusion | bytes 6136 | tf_op jit(solution)/shard_map/jit(_take)/gather | solution.py:56
  64.0 4.0 %gather_fusion.12 = f32[118,6]{1,0:T(8,128)S(1)} fusion(f32[6,16384]{0,1:T(8,128)} %copy.74, s32[1024]{0:T(1024)S(1)} %get-tuple-element.95), kind=kCustom, calls=%fused_computation.12.clone | custom fusion | bytes 6136 | tf_op jit(solution)/shard_map/jit(_take)/gather | solution.py:56
  68.1 4.0 %gather_fusion.15 = f32[118,6]{1,0:T(8,128)S(1)} fusion(f32[6,16384]{0,1:T(8,128)} %copy.74, s32[1024]{0:T(1024)S(1)} %get-tuple-element.92), kind=kCustom, calls=%fused_computation.15.clone | custom fusion | bytes 6136 | tf_op jit(solution)/shard_map/jit(_take)/gather | solution.py:56
  72.2 4.0 %gather_fusion.1 = f32[118,6]{1,0:T(8,128)S(1)} fusion(f32[6,16384]{0,1:T(8,128)} %copy.74, s32[1024]{0:T(1024)S(1)} %pad_clamp_fusion.15), kind=kCustom, calls=%fused_computation.1.clone | custom fusion | bytes 6136 | tf_op jit(solution)/shard_map/jit(_take)/gather | solution.py:56
  76.3 4.0 %gather_fusion = f32[118,6]{1,0:T(8,128)S(1)} fusion(f32[6,16384]{0,1:T(8,128)} %copy.74, s32[1024]{0:T(1024)S(1)} %pad_clamp_fusion.16), kind=kCustom, calls=%fused_computation.clone | custom fusion | bytes 6136 | tf_op jit(solution)/shard_map/jit(_take)/gather | solution.py:56
  80.5 4.0 %collective-permute-start = (f32[6,1,118]{2,0,1:T(8,128)S(1)}, f32[6,1,118]{2,0,1:T(8,128)S(1)}, u32[]{:S(2)}, u32[]{:S(2)}) collective-permute-start(f32[6,1,118]{2,0,1:T(8,128)S(1)} %fusion.14), channel_id=1, source_target_pairs={{0,384},{384,0},{1,385},{385,1},{2,386},{386,2},{3,387},{387,3},{4... | collective-permute-start | bytes 8504 | tf_op jit(solution)/shard_map/ppermute | solution.py:27
  84.5 4.0 %collective-permute-start.1 = (f32[1,3,2,2,128]{4,3,2,1,0:T(2,128)S(1)}, f32[1,3,2,2,128]{4,3,2,1,0:T(2,128)S(1)}, u32[]{:S(2)}, u32[]{:S(2)}) collective-permute-start(f32[1,3,2,2,128]{4,3,2,1,0:T(2,128)S(1)} %get-tuple-element.40), channel_id=1, source_target_pairs={{0,32},{32,64},{64,96},{96,128},{128,160},{160,192},{192,224},{224... | collective-permute-start | bytes 18440 | tf_op jit(solution)/shard_map/ppermute | solution.py:14
  88.5 1.3 collective-permute-start.2
  91.9 3.7 %scatter_custom_fusion = f32[16384]{0:T(1024)S(1)} fusion(s32[508]{0:T(512)S(1)} %bitcast.247, f32[508]{0:T(512)S(1)} %fusion.29, f32[]{:T(128)} %constant.41.clone.1), kind=kCustom, calls=%fused_computation.41 | custom fusion | flops 508 | bytes 65540 | tf_op jit(solution)/shard_map/scatter-add | solution.py:102
  96.1 4.3 %collective-permute-start.3 = (f32[1,3,2,132,2]{4,3,2,1,0:T(8,128)S(1)}, f32[1,3,2,132,2]{4,3,2,1,0:T(8,128)S(1)}, u32[]{:S(2)}, u32[]{:S(2)}) collective-permute-start(f32[1,3,2,132,2]{4,3,2,1,0:T(8,128)S(1)} %get-tuple-element.38), channel_id=1, source_target_pairs={{0,1},{1,2},{2,3},{3,4},{4,5},{5,6},{6,7},{7,8},{8,9},{9,10},{10,1... | collective-permute-start | bytes 19016 | tf_op jit(solution)/shard_map/ppermute | solution.py:14
  100.3 4.5 %collective-permute-start.4 = (f32[1,3,2,132,2]{4,3,2,1,0:T(8,128)S(1)}, f32[1,3,2,132,2]{4,3,2,1,0:T(8,128)S(1)}, u32[]{:S(2)}, u32[]{:S(2)}) collective-permute-start(f32[1,3,2,132,2]{4,3,2,1,0:T(8,128)S(1)} %get-tuple-element.39), channel_id=1, source_target_pairs={{1,0},{2,1},{3,2},{4,3},{5,4},{6,5},{7,6},{8,7},{9,8},{10,9},{11,1... | collective-permute-start | bytes 19016 | tf_op jit(solution)/shard_map/ppermute | solution.py:15
  105.3 4.4 %collective-permute-done.4 = f32[1,3,2,132,2]{4,3,2,1,0:T(8,128)S(1)} collective-permute-done((f32[1,3,2,132,2]{4,3,2,1,0:T(8,128)S(1)}, f32[1,3,2,132,2]{4,3,2,1,0:T(8,128)S(1)}, u32[]{:S(2)}, u32[]{:S(2)}) %collective-permute-start.4) | collective-permute-done | bytes 6368 | tf_op jit(solution)/shard_map/ppermute | solution.py:15
  111.2 5.4 %copy.108 = f32[6,16384]{0,1:T(8,128)} copy(f32[6,16384]{1,0:T(8,128)S(1)} %bitcast.241) | data formatting | bytes 786432 | tf_op jit(solution)/shard_map/reshape | solution.py:92
  116.5 143.0 %all-gather.2.cloned.1.call-done = f32[6,384,118]{2,0,1:T(8,128)} async-done(((f32[6,1,118]{2,0,1:T(8,128)}), f32[6,384,118]{2,0,1:T(8,128)}) %all-gather.2.cloned.1.call-update) | async-done | bytes 1087504 | tf_op jit(solution)/shard_map/all_gather | solution.py:97
  259.5 1.6 copy.106
  262.3 11.9 %copy.107 = f32[6,45312]{0,1:T(8,128)} copy(f32[6,45312]{1,0:T(8,128)S(1)} %reshape.171) | data formatting | bytes 2174976 | tf_op jit(solution)/shard_map/reshape | solution.py:66
  274.2 9.1 %scatter_custom_fusion.1 = f32[6,16384]{0,1:T(8,128)} fusion(s32[508]{0:T(512)S(1)} %bitcast.248, f32[]{:T(128)} %constant.41.clone.1, f32[508]{0:T(512)S(1)} %fusion.29, f32[]{:T(128)} %constant.92.clone.1, pred[508]{0:T(512)(128)(4,1)S(1)} %and_reduce_fusion, pred[508]{0:T(512)(128)(4,1)S(1)} %compare_and_fusion.16, f32[6,45312]{0,1:T(8,128)} %copy.107, ...), kind=kCustom, calls=%fused_computation.19 | custom fusion | flops 12192 | bytes 23601664 | tf_op jit(solution)/shard_map/scatter-add | solution.py:101
  283.3 10.7 %broadcast_select_fusion = f32[6,16384]{0,1:T(8,128)} fusion(f32[6,16384]{0,1:T(8,128)} %scatter_custom_fusion.1, f32[6,16384]{0,1:T(8,128)} %copy.108, pred[16384]{0:T(1024)(128)(4,1)S(1)} %broadcast_compare_fusion), kind=kLoop, calls=%fused_computation.21 | loop fusion | flops 98304 | bytes 1196032 | tf_op jit(solution)/shard_map/jit(_where)/select_n | solution.py:103
  294.1 5.7 %copy.109 = f32[6,16384]{1,0:T(8,128)S(1)} copy(f32[6,16384]{0,1:T(8,128)} %broadcast_select_fusion) | data formatting | bytes 786432 | tf_op jit(solution)/shard_map/jit(_where)/select_n | solution.py:103
  (70 shorter events, 9.1 us)
Async XLA Ops:
  6.5 78.0 %copy-start = (f32[1,3,2,128,128]{4,3,2,1,0:T(8,128)S(1)}, f32[1,3,2,128,128]{4,3,2,1,0:T(8,128)}, u32[]{:S(2)}) copy-start(f32[1,3,2,128,128]{4,3,2,1,0:T(8,128)} %param.10) | copy-start | bytes 1179652
  6.5 73.9 %copy-start.2 = (f32[1,1,1,16,118]{4,3,2,1,0:T(8,128)S(1)}, f32[1,1,1,16,118]{4,3,2,1,0:T(8,128)}, u32[]{:S(2)}) copy-start(f32[1,1,1,16,118]{4,3,2,1,0:T(8,128)} %param.14) | copy-start | bytes 22660
  6.5 83.3 %copy-start.5 = (s32[1,1,1,508]{3,2,1,0:T(1,128)S(1)}, s32[1,1,1,508]{3,2,1,0:T(1,128)}, u32[]{:S(2)}) copy-start(s32[1,1,1,508]{3,2,1,0:T(1,128)} %param.17) | copy-start | bytes 6100
  6.5 83.3 %copy-start.7 = (f32[3]{0:T(128)S(1)}, f32[3]{0:T(128)}, u32[]{:S(2)}) copy-start(f32[3]{0:T(128)} %param.12) | copy-start | bytes 40
  6.5 89.1 %copy-start.3 = (s32[1,1,1,508]{3,2,1,0:T(1,128)S(1)}, s32[1,1,1,508]{3,2,1,0:T(1,128)}, u32[]{:S(2)}) copy-start(s32[1,1,1,508]{3,2,1,0:T(1,128)} %param.15) | copy-start | bytes 6100
  6.5 89.1 %copy-start.6 = (s32[1,1,1,508]{3,2,1,0:T(1,128)S(1)}, s32[1,1,1,508]{3,2,1,0:T(1,128)}, u32[]{:S(2)}) copy-start(s32[1,1,1,508]{3,2,1,0:T(1,128)} %param.16) | copy-start | bytes 6100
  6.6 89.2 %copy-start.1 = (f32[1,2,2,128,128]{4,3,2,1,0:T(8,128)S(1)}, f32[1,2,2,128,128]{4,3,2,1,0:T(8,128)}, u32[]{:S(2)}) copy-start(f32[1,2,2,128,128]{4,3,2,1,0:T(8,128)} %param.11) | copy-start | bytes 786436
  6.6 252.9 %all-gather.2.cloned.1.call-start = ((), (), s32[]{:S(2)}) async-start(), calls=%async_computation | async-start | bytes 1576960 | tf_op jit(solution)/shard_map/all_gather | solution.py:97
  80.5 10.2 %collective-permute-start = (f32[6,1,118]{2,0,1:T(8,128)S(1)}, f32[6,1,118]{2,0,1:T(8,128)S(1)}, u32[]{:S(2)}, u32[]{:S(2)}) collective-permute-start(f32[6,1,118]{2,0,1:T(8,128)S(1)} %fusion.14), channel_id=1, source_target_pairs={{0,384},{384,0},{1,385},{385,1},{2,386},{386,2},{3,387},{387,3},{4... | collective-permute-start | bytes 8504 | tf_op jit(solution)/shard_map/ppermute | solution.py:27
  84.5 11.3 %collective-permute-start.1 = (f32[1,3,2,2,128]{4,3,2,1,0:T(2,128)S(1)}, f32[1,3,2,2,128]{4,3,2,1,0:T(2,128)S(1)}, u32[]{:S(2)}, u32[]{:S(2)}) collective-permute-start(f32[1,3,2,2,128]{4,3,2,1,0:T(2,128)S(1)} %get-tuple-element.40), channel_id=1, source_target_pairs={{0,32},{32,64},{64,96},{96,128},{128,160},{160,192},{192,224},{224... | collective-permute-start | bytes 18440 | tf_op jit(solution)/shard_map/ppermute | solution.py:14
  88.5 7.3 %collective-permute-start.2 = (f32[1,3,2,2,128]{4,3,2,1,0:T(2,128)S(1)}, f32[1,3,2,2,128]{4,3,2,1,0:T(2,128)S(1)}, u32[]{:S(2)}, u32[]{:S(2)}) collective-permute-start(f32[1,3,2,2,128]{4,3,2,1,0:T(2,128)S(1)} %get-tuple-element.41), channel_id=1, source_target_pairs={{32,0},{64,32},{96,64},{128,96},{160,128},{192,160},{224,192},{256... | collective-permute-start | bytes 18440 | tf_op jit(solution)/shard_map/ppermute | solution.py:15
  90.7 0.6 copy-start.4
  96.1 9.2 %collective-permute-start.3 = (f32[1,3,2,132,2]{4,3,2,1,0:T(8,128)S(1)}, f32[1,3,2,132,2]{4,3,2,1,0:T(8,128)S(1)}, u32[]{:S(2)}, u32[]{:S(2)}) collective-permute-start(f32[1,3,2,132,2]{4,3,2,1,0:T(8,128)S(1)} %get-tuple-element.38), channel_id=1, source_target_pairs={{0,1},{1,2},{2,3},{3,4},{4,5},{5,6},{6,7},{7,8},{8,9},{9,10},{10,1... | collective-permute-start | bytes 19016 | tf_op jit(solution)/shard_map/ppermute | solution.py:14
  100.3 9.4 %collective-permute-start.4 = (f32[1,3,2,132,2]{4,3,2,1,0:T(8,128)S(1)}, f32[1,3,2,132,2]{4,3,2,1,0:T(8,128)S(1)}, u32[]{:S(2)}, u32[]{:S(2)}) collective-permute-start(f32[1,3,2,132,2]{4,3,2,1,0:T(8,128)S(1)} %get-tuple-element.39), channel_id=1, source_target_pairs={{1,0},{2,1},{3,2},{4,3},{5,4},{6,5},{7,6},{8,7},{9,8},{10,9},{11,1... | collective-permute-start | bytes 19016 | tf_op jit(solution)/shard_map/ppermute | solution.py:15
Sparse Core Ops, SparseCore 0:
  91.4 168.0 all-gather.1
where the time goes:
time: 308 us; the launch traced here: 307 us
  waiting for transfers between devices  148 us (48%)
  local copies, waits for them, and re-layouts  99.8 us (32%)
  other arithmetic  28 us (9%)
  starting transfers between devices  18.1 us (6%)
  between operations  13.7 us (4%)
    all_gather x1, waiting for transfers between devices, per_device(): lax.all_gather(crossed, ('lat', 'lon'), axis=1, tiled=True)  143 us
    gather x32, local copies, waits for them, and re-layouts, interpolate(): picked = jnp.take(flattened, corners + vertical * breadth + lateral, axis=1)  65.6 us
    reshape x2, local copies, waits for them, and re-layouts, pick_rows(): flattened_piece = piece.reshape(piece.shape[0], piece_count * slot_count)  13.1 us
    select_n x1, other arithmetic, per_device(): result = jnp.where(presence[None, :] > 0.5, landed, advanced)  10.7 us
    scatter-add x1, other arithmetic, per_device(): jnp.zeros((channels, height * breadth), jnp.float32).at[:, receptor_cells]  9.15 us
    ppermute x2, starting transfers between devices, with_halo(): before = lax.ppermute(last, axis, up)  8.26 us
  transfers between devices with their start and end apart: 6, of which 3 were waited for; matrix products, arithmetic and copies ran while one was open for 4% of the time, Pallas kernels for 0%

commit v1 on v0

v1 whole, which is shorter than its diff:
```python
import functools

import jax
import jax.numpy as jnp
from jax import lax
from jax.experimental import pallas as pl
from jax.experimental.pallas import tpu as pltpu
from jax.sharding import PartitionSpec as P

LANES = 128
BF16 = jnp.bfloat16
F32 = jnp.float32
NT = (((1,), (1,)), ((), ()))
VMEM = pl.BlockSpec(memory_space=pltpu.VMEM)
SMEM = pl.BlockSpec(memory_space=pltpu.SMEM)


def position():
    lat, lats = lax.axis_index("lat"), lax.axis_size("lat")
    lon, lons = lax.axis_index("lon"), lax.axis_size("lon")
    return lat, lats, lon, lons


def halves(values):
    high = values.astype(BF16)
    low = (values - high.astype(F32)).astype(BF16)
    return jnp.concatenate([high, low], axis=1)


def ask_kernel(tile_ref, slot_ref, cell_ref, field_ref, out_ref, key_ref, value_ref):
    lat, lats, lon, lons = position()
    channels, height, breadth = field_ref.shape
    cap = cell_ref.shape[1]
    edge_rows = 2 * ((lat == 0).astype(jnp.int32) + (lat == lats - 1).astype(jnp.int32))
    edge_cols = 2 * ((lon == 0).astype(jnp.int32) + (lon == lons - 1).astype(jnp.int32))
    count = edge_rows * breadth + edge_cols * height - edge_rows * edge_cols
    live = lax.broadcasted_iota(jnp.int32, (1, cap), 1) < count
    tile = tile_ref[...]
    key_ref[...] = jnp.full(key_ref.shape, -1, jnp.int32)
    value_ref[...] = jnp.zeros(value_ref.shape, F32)
    key_ref[:, :cap] = jnp.where(live, cell_ref[...], -1)
    value_ref[0:1, :cap] = (tile // lons + 1).astype(F32)
    value_ref[1:2, :cap] = (tile % lons).astype(F32)
    value_ref[2:3, :cap] = slot_ref[...].astype(F32)
    row0 = jnp.where(lat == 0, 0, height - 2)
    col0 = jnp.where(lon == 0, 0, breadth - 2)
    across = lax.broadcasted_iota(jnp.int32, (breadth, LANES), 0)
    down = lax.broadcasted_iota(jnp.int32, (height, LANES), 0)
    cells = jnp.concatenate(
        [
            row0 * breadth + across,
            (row0 + 1) * breadth + across,
            down * breadth + col0,
            down * breadth + col0 + 1,
        ],
        axis=0,
    )
    found = jnp.zeros((8, 4 * LANES), F32)
    for group in range(key_ref.shape[1] // LANES):
        span = slice(group * LANES, (group + 1) * LANES)
        hit = jnp.where(cells == key_ref[:, span], 1.0, 0.0).astype(BF16)
        found = found + lax.dot_general(
            value_ref[:, span].astype(BF16), hit, NT, preferred_element_type=F32
        )
    wanted = (found[0:1] - 1.0) * lons + found[1:2]
    for strip in range(4):
        span = slice(strip * LANES, (strip + 1) * LANES)
        out_ref[0, strip : strip + 1, :] = wanted[:, span]
        out_ref[0, 4 + strip : 5 + strip, :] = found[2:3, span]
    block = out_ref[0, 0:8, :]
    for other in range(1, lats):
        out_ref[other, 0:8, :] = block

    @pl.when(lat > 0)
    def _():
        for ch in range(channels):
            out_ref[lat - 1, 8 + 2 * ch : 10 + 2 * ch, :] = field_ref[ch, 0:2, :]

    @pl.when(lat < lats - 1)
    def _():
        for ch in range(channels):
            out_ref[lat + 1, 8 + 2 * ch : 10 + 2 * ch, :] = field_ref[ch, height - 2 : height, :]


def donate_kernel(cell_ref, weight_ref, field_ref, out_ref, corner_ref, padded_ref):
    lat, lats, lon, lons = position()
    panel = lax.axis_index("panel")
    channels, height, breadth = field_ref.shape
    cap = cell_ref.shape[1]
    corner_ref[...] = jnp.zeros(corner_ref.shape, jnp.int32)
    padded_ref[...] = jnp.zeros(padded_ref.shape, F32)
    corner_ref[:, :cap] = cell_ref[...]
    padded_ref[:, :cap] = weight_ref[...]
    corner = corner_ref[...]
    upper, left = corner // breadth, corner % breadth
    index = lax.broadcasted_iota(jnp.int32, (LANES, LANES), 0)
    columns = []
    weights = []
    for lateral in range(4):
        columns.append(jnp.where(index == left + lateral, 1.0, 0.0).astype(BF16))
        spread = jnp.zeros((height, LANES), F32)
        for vertical in range(4):
            k = 4 * vertical + lateral
            spread = jnp.where(index == upper + vertical, padded_ref[k : k + 1, :], spread)
        weights.append(spread)
    picker = jnp.concatenate(columns, axis=1)
    picker = jnp.concatenate([picker, picker], axis=0)
    base = (1 - panel) * lons
    rows = []
    for ch in range(channels):
        along = lax.dot(halves(field_ref[ch]), picker, preferred_element_type=F32)
        total = jnp.zeros((height, LANES), F32)
        for lateral in range(4):
            total = total + along[:, lateral * LANES : (lateral + 1) * LANES] * weights[lateral]
        rows.append(jnp.sum(total, axis=0, keepdims=True))
    rows.append(jnp.zeros((8 - channels, LANES), F32))
    block = jnp.concatenate(rows, axis=0)
    for other in range(lons):
        out_ref[base + other, 0:8, :] = block

    lane = lax.broadcasted_iota(jnp.int32, (height, LANES), 1)
    edges = jnp.zeros((height, LANES), F32)
    for ch in range(channels):
        state = field_ref[ch]
        first = state if ch == 0 else pltpu.roll(state, 2 * ch, 1)
        last = pltpu.roll(state, 2 * channels + 2 * ch + 2, 1)
        edges = jnp.where(lane // 2 == ch, first, edges)
        edges = jnp.where(lane // 2 == channels + ch, last, edges)
    edges = edges.T

    @pl.when(lon > 0)
    def _():
        out_ref[panel * lons + lon - 1, 0 : 2 * channels, :] = edges[0 : 2 * channels]

    @pl.when(lon < lons - 1)
    def _():
        out_ref[panel * lons + lon + 1, 0 : 2 * channels, :] = edges[2 * channels : 4 * channels]


def pick_kernel(asked_ref, given_ref, out_ref):
    lat, lats, lon, lons = position()
    panel = lax.axis_index("panel")
    given = given_ref[pl.ds((1 - panel) * lons, lons), 0:8, :].reshape(lons * 8, LANES)
    given = halves(given)
    first = (lat * lons).astype(F32)
    index = lax.broadcasted_iota(jnp.int32, (LANES, 2 * LANES), 0).astype(F32)

    def pick(other, strip):
        tile = jnp.concatenate(
            [asked_ref[other, strip : strip + 1, :], asked_ref[other, strip + 1 : strip + 2, :]], axis=1
        )
        slot = jnp.concatenate(
            [asked_ref[other, 4 + strip : 5 + strip, :], asked_ref[other, 5 + strip : 6 + strip, :]], axis=1
        )
        hit = jnp.where(index == slot, 1.0, 0.0).astype(BF16)
        hit = jnp.concatenate([hit, hit], axis=0)
        values = lax.dot(given, hit, preferred_element_type=F32)
        place = tile - first
        total = jnp.zeros((8, 2 * LANES), F32)
        for donor in range(lons):
            total = total + jnp.where(place == float(donor), values[donor * 8 : donor * 8 + 8], 0.0)
        out_ref[other, strip * 8 : strip * 8 + 8, :] = total[:, :LANES]
        out_ref[other, strip * 8 + 8 : strip * 8 + 16, :] = total[:, LANES:]

    pick(0, 0)
    pick(lats - 1, 0)

    @pl.when((lon == 0) | (lon == lons - 1))
    def _():
        for other in range(lats):
            pick(other, 2)


def advance_kernel(diffusion_ref, field_ref, velocity_ref, asked_ref, given_ref, out_ref, tall_ref, side_ref):
    lat, lats, lon, lons = position()
    panel = lax.axis_index("panel")
    channels, height, breadth = field_ref.shape
    radii = velocity_ref.shape[0] // 2
    width = 2 * channels
    above = asked_ref[jnp.maximum(lat - 1, 0), 8 : 8 + width, :]
    below = asked_ref[jnp.minimum(lat + 1, lats - 1), 8 : 8 + width, :]
    above = jnp.where(lat > 0, above, 0.0)
    below = jnp.where(lat < lats - 1, below, 0.0)
    before = given_ref[panel * lons + jnp.maximum(lon - 1, 0), 0:width, :]
    after = given_ref[panel * lons + jnp.minimum(lon + 1, lons - 1), 0:width, :]
    side_ref[...] = jnp.zeros(side_ref.shape, F32)
    side_ref[0:width, :] = jnp.where(lon > 0, before, 0.0)
    side_ref[width : 2 * width, :] = jnp.where(lon < lons - 1, after, 0.0)
    sides = side_ref[...].T
    lane = lax.broadcasted_iota(jnp.int32, (height, breadth), 1)
    for ch in range(channels):
        state = field_ref[ch]
        tall_ref[ch, 6:8, :] = above[2 * ch : 2 * ch + 2]
        tall_ref[ch, 8 : 8 + height, :] = state
        tall_ref[ch, 8 + height : 10 + height, :] = below[2 * ch : 2 * ch + 2]
        up2 = tall_ref[ch, 6 : 6 + height, :]
        up1 = tall_ref[ch, 7 : 7 + height, :]
        down1 = tall_ref[ch, 9 : 9 + height, :]
        down2 = tall_ref[ch, 10 : 10 + height, :]
        left = pltpu.roll(sides, breadth - 2 - 2 * ch, 1)
        right = pltpu.roll(sides, breadth - width - 2 * ch, 1)
        left2 = pltpu.roll(jnp.where(lane >= breadth - 2, left, state), 2, 1)
        left1 = pltpu.roll(jnp.where(lane >= breadth - 1, left, state), 1, 1)
        right1 = pltpu.roll(jnp.where(lane < 1, right, state), breadth - 1, 1)
        right2 = pltpu.roll(jnp.where(lane < 2, right, state), breadth - 2, 1)
        slope_th = (up2 - down2 + 8.0 * (down1 - up1)) * (1.0 / 12.0)
        slope_ph = (left2 - right2 + 8.0 * (right1 - left1)) * (1.0 / 12.0)
        near = (down1 + up1) + (right1 + left1)
        far = (down2 + up2) + (right2 + left2)
        curve = (16.0 * near - far - 60.0 * state) * (1.0 / 12.0)
        carried = velocity_ref[ch % radii] * slope_th + velocity_ref[radii + ch % radii] * slope_ph
        out_ref[ch] = state - carried + diffusion_ref[ch // radii] * curve


def land_kernel(advanced_ref, taken_ref, out_ref, side_ref):
    lat, lats, lon, lons = position()
    channels, height, breadth = advanced_ref.shape
    out_ref[...] = advanced_ref[...]

    def strip(which):
        total = taken_ref[0, which * 8 : which * 8 + 8, :]
        for other in range(1, lats):
            total = total + taken_ref[other, which * 8 : which * 8 + 8, :]
        return total

    @pl.when((lon == 0) | (lon == lons - 1))
    def _():
        side_ref[...] = jnp.zeros(side_ref.shape, F32)
        side_ref[0:8, :] = strip(2)
        side_ref[8:16, :] = strip(3)
        sides = side_ref[...].T
        lane = lax.broadcasted_iota(jnp.int32, (height, breadth), 1)
        col0 = jnp.where(lon == 0, 0, breadth - 2)
        for ch in range(channels):
            block = out_ref[ch]
            block = jnp.where(lane == col0, sides[:, ch : ch + 1], block)
            block = jnp.where(lane == col0 + 1, sides[:, 8 + ch : 9 + ch], block)
            out_ref[ch] = block

    @pl.when((lat == 0) | (lat == lats - 1))
    def _():
        row0 = jnp.where(lat == 0, 0, height - 2)
        for which in range(2):
            values = strip(which)
            for ch in range(channels):
                out_ref[ch, pl.ds(row0 + which, 1), :] = values[ch : ch + 1]


def per_device(
    field, velocity, diffusion, donor_cell, donor_weight, source_tile, source_slot, recv_cell
):
    _, fields, radii, height, breadth = field.shape
    channels = fields * radii
    lats = lax.axis_size("lat")
    lons = lax.axis_size("lon")
    state = field.reshape(channels, height, breadth)
    speed = velocity.reshape(2 * radii, height, breadth)
    corners = donor_cell.reshape(1, -1)
    weights = donor_weight.reshape(16, -1)
    tiles = source_tile.reshape(1, -1)
    slots = source_slot.reshape(1, -1)
    cells = recv_cell.reshape(1, -1)
    padded = -(-cells.shape[1] // LANES) * LANES

    asked = pl.pallas_call(
        ask_kernel,
        out_shape=jax.ShapeDtypeStruct((lats, 24, LANES), F32),
        in_specs=[VMEM] * 4,
        out_specs=VMEM,
        scratch_shapes=[pltpu.VMEM((1, padded), jnp.int32), pltpu.VMEM((8, padded), F32)],
        name="ask",
    )(tiles, slots, cells, state)
    asked = lax.all_to_all(asked, "lat", 0, 0, tiled=True)

    given = pl.pallas_call(
        donate_kernel,
        out_shape=jax.ShapeDtypeStruct((2 * lons, 16, LANES), F32),
        in_specs=[VMEM] * 3,
        out_specs=VMEM,
        scratch_shapes=[pltpu.VMEM((1, LANES), jnp.int32), pltpu.VMEM((16, LANES), F32)],
        cost_estimate=pl.CostEstimate(flops=400_000_000, bytes_accessed=1_000_000, transcendentals=0),
        name="donate",
    )(corners, weights, state)
    given = lax.all_to_all(given, ("panel", "lon"), 0, 0, tiled=True)

    taken = pl.pallas_call(
        pick_kernel,
        out_shape=jax.ShapeDtypeStruct((lats, 32, LANES), F32),
        in_specs=[VMEM] * 2,
        out_specs=VMEM,
        name="pick",
    )(asked, given)
    taken = lax.all_to_all(taken, "lat", 0, 0, tiled=True)

    advanced = pl.pallas_call(
        advance_kernel,
        out_shape=jax.ShapeDtypeStruct((channels, height, breadth), F32),
        in_specs=[SMEM] + [VMEM] * 4,
        out_specs=VMEM,
        scratch_shapes=[
            pltpu.VMEM((channels, height + 16, breadth), F32),
            pltpu.VMEM((LANES, LANES), F32),
        ],
        cost_estimate=pl.CostEstimate(flops=4_000_000, bytes_accessed=2_000_000, transcendentals=0),
        name="advance",
    )(diffusion, state, speed, asked, given)

    stepped = pl.pallas_call(
        land_kernel,
        out_shape=jax.ShapeDtypeStruct((channels, height, breadth), F32),
        in_specs=[VMEM] * 2,
        out_specs=VMEM,
        scratch_shapes=[pltpu.VMEM((LANES, LANES), F32)],
        name="land",
    )(advanced, taken)
    return stepped.reshape(field.shape)


def solution(mesh):
    placed = (
        P("panel", None, None, "lat", "lon"),
        P("panel", None, None, "lat", "lon"),
        P(),
        P("panel", "lat", "lon", None),
        P("panel", "lat", "lon", None, None),
        P("panel", "lat", "lon", None),
        P("panel", "lat", "lon", None),
        P("panel", "lat", "lon", None),
    )
    return jax.shard_map(
        per_device,
        mesh=mesh,
        in_specs=placed,
        out_specs=P("panel", None, None, "lat", "lon"),
        check_vma=False,
    )
```

time: 308 us -> 82.6 us (0.27)
  the two profiles are of different devices: /device:TPU:1 before, /device:TPU:8 now
where the time goes in v1:
time: 82.6 us; the launch traced here: 82.2 us
  blocking collectives  29.6 us (36%)
  waiting for transfers between devices  20.7 us (25%)
  starting transfers between devices  18.7 us (23%)
  Pallas kernels  12.4 us (15%)
    all_to_all x1, blocking collectives, per_device(): given = lax.all_to_all(given, ('panel', 'lon'), 0, 0, tiled=True)  29.6 us
    all_to_all x1, starting transfers between devices, per_device(): asked = lax.all_to_all(asked, 'lat', 0, 0, tiled=True)  15.2 us
    all_to_all x1, waiting for transfers between devices, per_device(): asked = lax.all_to_all(asked, 'lat', 0, 0, tiled=True)  10.6 us
    all_to_all x1, waiting for transfers between devices, per_device(): taken = lax.all_to_all(taken, 'lat', 0, 0, tiled=True)  10.2 us
    all_to_all x1, starting transfers between devices, per_device(): taken = lax.all_to_all(taken, 'lat', 0, 0, tiled=True)  3.53 us
    pallas_call x1, Pallas kernels, per_device(): pl.pallas_call(advance_kernel, out_shape=jax.ShapeDtypeStruct((channels,...  2.95 us
    pallas_call x1, Pallas kernels, per_device(): pl.pallas_call(pick_kernel, out_shape=jax.ShapeDtypeStruct((lats, 32, LAN...  2.92 us
    pallas_call x1, Pallas kernels, per_device(): pl.pallas_call(donate_kernel, out_shape=jax.ShapeDtypeStruct((2 * lons, 1...  2.28 us
  transfers between devices with their start and end apart: 2, of which 2 were waited for; matrix products, arithmetic and copies ran while one was open for 0% of the time, Pallas kernels for 6%

profile of v1, /device:TPU:8, one launch (start us, length us, event | category | flops | bytes accessed | tf_op | source)
XLA Modules:
  0.0 82.2 jit_solution(17917593031886764059)
XLA Ops:
  0.0 2.0 %ask.1 = f32[12,24,128]{2,1,0:T(8,128)} custom-call(s32[1,508]{1,0:T(1,128)} %bitcast.12, s32[1,508]{1,0:T(1,128)} %bitcast.13, s32[1,508]{1,0:T(1,128)} %bitcast.14, f32[6,128,128]{2,1,0:T(8,128)} %bitcast.8), custom_call_target="tpu_custom_call" | custom-call | tf_op jit(solution)/shard_map/ask/pallas_call | solution.py:265
  2.0 15.2 %all-to-all-start = ((f32[12,24,128]{2,1,0:T(8,128)}), f32[12,24,128]{2,1,0:T(8,128)S(1)}, u32[]{:S(2)}, u32[]{:S(2)}) async-start(f32[12,24,128]{2,1,0:T(8,128)} %ask.1), calls=%async_computation | async-start | bytes 294912 | tf_op jit(solution)/shard_map/all_to_all | solution.py:273
  17.2 2.3 %donate.1 = f32[64,16,128]{2,1,0:T(8,128)} custom-call(s32[1,118]{1,0:T(1,128)} %bitcast.16, f32[16,118]{1,0:T(8,128)} %bitcast.15, f32[6,128,128]{2,1,0:T(8,128)} %bitcast.9), custom_call_target="tpu_custom_call" | custom-call | flops 400000000 | bytes 1000000 | tf_op jit(solution)/shard_map/donate/pallas_call | solution.py:275
  19.5 10.6 %all-to-all-done.asked_ref = f32[12,24,128]{2,1,0:T(8,128)S(1)} async-done(((f32[12,24,128]{2,1,0:T(8,128)}), f32[12,24,128]{2,1,0:T(8,128)S(1)}, u32[]{:S(2)}, u32[]{:S(2)}) %all-to-all-start) | async-done | bytes 147488 | tf_op jit(solution)/shard_map/all_to_all | solution.py:273
  30.1 0.0 copy-start
  30.1 29.6 %all_to_all.15.given_ref = f32[64,16,128]{2,1,0:T(8,128)} all-to-all(f32[64,16,128]{2,1,0:T(8,128)} %donate.1), channel_id=1, replica_groups=mesh['panel'=2,'lat'=12,'lon'=32] {'panel','lon'}, dimensions={0} | all-to-all | bytes 1048576 | tf_op jit(solution)/shard_map/all_to_all | solution.py:284
  59.7 0.0 copy-done
  59.7 2.9 %pick.1 = f32[12,32,128]{2,1,0:T(8,128)} custom-call(f32[12,24,128]{2,1,0:T(8,128)} %copy-done, f32[64,16,128]{2,1,0:T(8,128)} %all_to_all.15.given_ref), custom_call_target="tpu_custom_call" | custom-call | tf_op jit(solution)/shard_map/pick/pallas_call | solution.py:286
  62.6 3.5 %all-to-all-start.2 = ((f32[12,32,128]{2,1,0:T(8,128)}), f32[12,32,128]{2,1,0:T(8,128)S(1)}, u32[]{:S(2)}, u32[]{:S(2)}) async-start(f32[12,32,128]{2,1,0:T(8,128)} %pick.1), calls=%async_computation.2 | async-start | bytes 393216 | tf_op jit(solution)/shard_map/all_to_all | solution.py:293
  66.1 3.0 %advance.1.advanced_ref = f32[6,128,128]{2,1,0:T(8,128)} custom-call(f32[3]{0:T(128)} %diffusion_ref.1, f32[6,128,128]{2,1,0:T(8,128)} %bitcast.10, f32[4,128,128]{2,1,0:T(8,128)} %bitcast.11, f32[12,24,128]{2,1,0:T(8,128)} %copy-done, f32[64,16,128]{2,1,0:T(8,128)} %all_to_all.15.given_ref), custom_call_target="tpu_custom_call" | custom-call | flops 4000000 | bytes 2000000 | tf_op jit(solution)/shard_map/advance/pallas_call | solution.py:295
  69.1 10.2 %all-to-all-done.2.taken_ref = f32[12,32,128]{2,1,0:T(8,128)S(1)} async-done(((f32[12,32,128]{2,1,0:T(8,128)}), f32[12,32,128]{2,1,0:T(8,128)S(1)}, u32[]{:S(2)}, u32[]{:S(2)}) %all-to-all-start.2) | async-done | bytes 196640 | tf_op jit(solution)/shard_map/all_to_all | solution.py:293
  79.2 0.0 copy-start.1
  79.3 0.7 copy-done.1
  79.9 2.2 %land.1 = f32[6,128,128]{2,1,0:T(8,128)} custom-call(f32[6,128,128]{2,1,0:T(8,128)} %advance.1.advanced_ref, f32[12,32,128]{2,1,0:T(8,128)} %copy-done.1), custom_call_target="tpu_custom_call" | custom-call | tf_op jit(solution)/shard_map/land/pallas_call | solution.py:308
Async XLA Ops:
  2.0 28.0 %all-to-all-start = ((f32[12,24,128]{2,1,0:T(8,128)}), f32[12,24,128]{2,1,0:T(8,128)S(1)}, u32[]{:S(2)}, u32[]{:S(2)}) async-start(f32[12,24,128]{2,1,0:T(8,128)} %ask.1), calls=%async_computation | async-start | bytes 294912 | tf_op jit(solution)/shard_map/all_to_all | solution.py:273
  30.1 29.6 %copy-start = (f32[12,24,128]{2,1,0:T(8,128)}, f32[12,24,128]{2,1,0:T(8,128)S(1)}, u32[]{:S(2)}) copy-start(f32[12,24,128]{2,1,0:T(8,128)S(1)} %all-to-all-done.asked_ref) | copy-start | bytes 442372
  62.6 16.6 %all-to-all-start.2 = ((f32[12,32,128]{2,1,0:T(8,128)}), f32[12,32,128]{2,1,0:T(8,128)S(1)}, u32[]{:S(2)}, u32[]{:S(2)}) async-start(f32[12,32,128]{2,1,0:T(8,128)} %pick.1), calls=%async_computation.2 | async-start | bytes 393216 | tf_op jit(solution)/shard_map/all_to_all | solution.py:293
  79.2 0.7 copy-start.1

commit v2 on v1

v2 whole, which is shorter than its diff:
```python
import functools

import jax
import jax.numpy as jnp
from jax import lax
from jax.experimental import pallas as pl
from jax.experimental.pallas import tpu as pltpu
from jax.sharding import Mesh
from jax.sharding import PartitionSpec as P

LANES = 128
BF16 = jnp.bfloat16
F32 = jnp.float32
NT = (((1,), (1,)), ((), ()))
VMEM = pl.BlockSpec(memory_space=pltpu.VMEM)
SMEM = pl.BlockSpec(memory_space=pltpu.SMEM)


GIVERS = ("lat", "high")
TAKERS = ("mid", "core")
LON = ("high", "mid", "core")


def position():
    lat, lats = lax.axis_index("lat"), lax.axis_size("lat")
    lon, lons = lax.axis_index(LON), lax.axis_size(LON)
    return lat, lats, lon, lons


def halves(values):
    high = values.astype(BF16)
    low = (values - high.astype(F32)).astype(BF16)
    return jnp.concatenate([high, low], axis=1)


def ask_kernel(tile_ref, slot_ref, cell_ref, out_ref, key_ref, value_ref, *, height, breadth):
    lat, lats, lon, lons = position()
    cap = cell_ref.shape[1]
    edge_rows = 2 * ((lat == 0).astype(jnp.int32) + (lat == lats - 1).astype(jnp.int32))
    edge_cols = 2 * ((lon == 0).astype(jnp.int32) + (lon == lons - 1).astype(jnp.int32))
    count = edge_rows * breadth + edge_cols * height - edge_rows * edge_cols
    live = lax.broadcasted_iota(jnp.int32, (1, cap), 1) < count
    parts = {}
    rest = tile_ref[...]
    for axis in reversed(("lat",) + LON):
        parts[axis] = rest % lax.axis_size(axis)
        rest = rest // lax.axis_size(axis)

    def along(axes):
        index = jnp.zeros((1, cap), jnp.int32)
        for axis in axes:
            index = index * lax.axis_size(axis) + parts[axis]
        return index

    key_ref[...] = jnp.full(key_ref.shape, -1, jnp.int32)
    value_ref[...] = jnp.zeros(value_ref.shape, F32)
    key_ref[:, :cap] = jnp.where(live, cell_ref[...], -1)
    value_ref[0:1, :cap] = along(GIVERS).astype(F32)
    value_ref[1:2, :cap] = (along(TAKERS) + 1).astype(F32)
    value_ref[2:3, :cap] = slot_ref[...].astype(F32)
    row0 = jnp.where(lat == 0, 0, height - 2)
    col0 = jnp.where(lon == 0, 0, breadth - 2)
    across = lax.broadcasted_iota(jnp.int32, (breadth, LANES), 0)
    down = lax.broadcasted_iota(jnp.int32, (height, LANES), 0)
    cells = jnp.concatenate(
        [
            row0 * breadth + across,
            (row0 + 1) * breadth + across,
            down * breadth + col0,
            down * breadth + col0 + 1,
        ],
        axis=0,
    )
    found = jnp.zeros((8, 4 * LANES), F32)
    for group in range(key_ref.shape[1] // LANES):
        span = slice(group * LANES, (group + 1) * LANES)
        hit = jnp.where(cells == key_ref[:, span], 1.0, 0.0).astype(BF16)
        found = found + lax.dot_general(
            value_ref[:, span].astype(BF16), hit, NT, preferred_element_type=F32
        )
    for other in range(out_ref.shape[0]):
        place = jnp.where(found[1:2] == float(other + 1), found[0:1], -1.0)
        for strip in range(4):
            span = slice(strip * LANES, (strip + 1) * LANES)
            out_ref[other, strip : strip + 1, :] = place[:, span]
            out_ref[other, 4 + strip : 5 + strip, :] = found[2:3, span]


def donate_kernel(cell_ref, weight_ref, field_ref, out_ref, corner_ref, padded_ref):
    channels, height, breadth = field_ref.shape
    cap = cell_ref.shape[1]
    corner_ref[...] = jnp.zeros(corner_ref.shape, jnp.int32)
    padded_ref[...] = jnp.zeros(padded_ref.shape, F32)
    corner_ref[:, :cap] = cell_ref[...]
    padded_ref[:, :cap] = weight_ref[...]
    corner = corner_ref[...]
    upper, left = corner // breadth, corner % breadth
    index = lax.broadcasted_iota(jnp.int32, (LANES, LANES), 0)
    columns = []
    weights = []
    for lateral in range(4):
        columns.append(jnp.where(index == left + lateral, 1.0, 0.0).astype(BF16))
        spread = jnp.zeros((height, LANES), F32)
        for vertical in range(4):
            k = 4 * vertical + lateral
            spread = jnp.where(index == upper + vertical, padded_ref[k : k + 1, :], spread)
        weights.append(spread)
    picker = jnp.concatenate(columns, axis=1)
    picker = jnp.concatenate([picker, picker], axis=0)
    out_ref[channels:, :] = jnp.zeros((8 - channels, LANES), F32)
    for ch in range(channels):
        along = lax.dot(halves(field_ref[ch]), picker, preferred_element_type=F32)
        total = along[:, :LANES] * weights[0]
        for lateral in range(1, 4):
            total = total + along[:, lateral * LANES : (lateral + 1) * LANES] * weights[lateral]
        out_ref[ch : ch + 1, :] = jnp.sum(total, axis=0, keepdims=True)


def edges_kernel(field_ref, top_ref, bottom_ref, first_ref, last_ref):
    channels, height, breadth = field_ref.shape
    lane = lax.broadcasted_iota(jnp.int32, (height, LANES), 1)
    edges = jnp.zeros((height, LANES), F32)
    for ch in range(channels):
        top_ref[2 * ch : 2 * ch + 2, :] = field_ref[ch, 0:2, :]
        bottom_ref[2 * ch : 2 * ch + 2, :] = field_ref[ch, height - 2 : height, :]
        state = field_ref[ch]
        first = state if ch == 0 else pltpu.roll(state, 2 * ch, 1)
        last = pltpu.roll(state, 2 * channels + 2 * ch + 2, 1)
        edges = jnp.where(lane // 2 == ch, first, edges)
        edges = jnp.where(lane // 2 == channels + ch, last, edges)
    edges = edges.T
    first_ref[...] = edges[0 : 2 * channels]
    last_ref[...] = edges[2 * channels : 4 * channels]


def pick_kernel(asked_ref, given_ref, out_ref):
    lat, lats, lon, lons = position()
    others = out_ref.shape[0]
    donors = given_ref.shape[0]
    given = halves(given_ref[...].reshape(donors * 8, LANES))
    index = lax.broadcasted_iota(jnp.int32, (LANES, 2 * LANES), 0).astype(F32)

    def pick(other, strip):
        place = jnp.concatenate(
            [asked_ref[other, strip : strip + 1, :], asked_ref[other, strip + 1 : strip + 2, :]], axis=1
        )
        slot = jnp.concatenate(
            [asked_ref[other, 4 + strip : 5 + strip, :], asked_ref[other, 5 + strip : 6 + strip, :]], axis=1
        )
        hit = jnp.where(index == slot, 1.0, 0.0).astype(BF16)
        hit = jnp.concatenate([hit, hit], axis=0)
        values = lax.dot(given, hit, preferred_element_type=F32)
        total = jnp.zeros((8, 2 * LANES), F32)
        for donor in range(donors):
            total = total + jnp.where(place == float(donor), values[donor * 8 : donor * 8 + 8], 0.0)
        out_ref[other, strip * 8 : strip * 8 + 8, :] = total[:, :LANES]
        out_ref[other, strip * 8 + 8 : strip * 8 + 16, :] = total[:, LANES:]

    out_ref[...] = jnp.zeros(out_ref.shape, F32)
    mine = lax.axis_index(TAKERS)

    @pl.when((lat == 0) | (lat == lats - 1))
    def _():
        for other in range(others):
            pick(other, 0)

    @pl.when(lon - longitude_part(mine) == 0)
    def _():
        pick(0, 2)

    @pl.when(lon - longitude_part(mine) + longitude_part(others - 1) == lons - 1)
    def _():
        pick(others - 1, 2)


def longitude_part(index):
    part = 0
    stride = {}
    step = 1
    for axis in reversed(LON):
        stride[axis] = step
        step = step * lax.axis_size(axis)
    for axis in reversed(TAKERS):
        size = lax.axis_size(axis)
        part = part + index % size * stride[axis]
        index = index // size
    return part


def advance_kernel(diffusion_ref, field_ref, velocity_ref, above_ref, below_ref, before_ref, after_ref, out_ref, tall_ref, side_ref):
    channels, height, breadth = field_ref.shape
    radii = velocity_ref.shape[0] // 2
    width = 2 * channels
    above = above_ref[...]
    below = below_ref[...]
    side_ref[...] = jnp.zeros(side_ref.shape, F32)
    side_ref[0:width, :] = before_ref[...]
    side_ref[width : 2 * width, :] = after_ref[...]
    sides = side_ref[...].T
    lane = lax.broadcasted_iota(jnp.int32, (height, breadth), 1)
    for ch in range(channels):
        state = field_ref[ch]
        tall_ref[ch, 6:8, :] = above[2 * ch : 2 * ch + 2]
        tall_ref[ch, 8 : 8 + height, :] = state
        tall_ref[ch, 8 + height : 10 + height, :] = below[2 * ch : 2 * ch + 2]
        up2 = tall_ref[ch, 6 : 6 + height, :]
        up1 = tall_ref[ch, 7 : 7 + height, :]
        down1 = tall_ref[ch, 9 : 9 + height, :]
        down2 = tall_ref[ch, 10 : 10 + height, :]
        left = pltpu.roll(sides, breadth - 2 - 2 * ch, 1)
        right = pltpu.roll(sides, breadth - width - 2 * ch, 1)
        left2 = pltpu.roll(jnp.where(lane >= breadth - 2, left, state), 2, 1)
        left1 = pltpu.roll(jnp.where(lane >= breadth - 1, left, state), 1, 1)
        right1 = pltpu.roll(jnp.where(lane < 1, right, state), breadth - 1, 1)
        right2 = pltpu.roll(jnp.where(lane < 2, right, state), breadth - 2, 1)
        slope_th = (up2 - down2 + 8.0 * (down1 - up1)) * (1.0 / 12.0)
        slope_ph = (left2 - right2 + 8.0 * (right1 - left1)) * (1.0 / 12.0)
        near = (down1 + up1) + (right1 + left1)
        far = (down2 + up2) + (right2 + left2)
        curve = (16.0 * near - far - 60.0 * state) * (1.0 / 12.0)
        carried = velocity_ref[ch % radii] * slope_th + velocity_ref[radii + ch % radii] * slope_ph
        out_ref[ch] = state - carried + diffusion_ref[ch // radii] * curve

def land_kernel(advanced_ref, taken_ref, out_ref, side_ref):
    lat, lats, lon, lons = position()
    channels, height, breadth = advanced_ref.shape
    out_ref[...] = advanced_ref[...]

    def strip(which):
        total = taken_ref[0, which * 8 : which * 8 + 8, :]
        for other in range(1, taken_ref.shape[0]):
            total = total + taken_ref[other, which * 8 : which * 8 + 8, :]
        return total

    @pl.when((lon == 0) | (lon == lons - 1))
    def _():
        side_ref[...] = jnp.zeros(side_ref.shape, F32)
        side_ref[0:8, :] = strip(2)
        side_ref[8:16, :] = strip(3)
        sides = side_ref[...].T
        lane = lax.broadcasted_iota(jnp.int32, (height, breadth), 1)
        col0 = jnp.where(lon == 0, 0, breadth - 2)
        for ch in range(channels):
            block = out_ref[ch]
            block = jnp.where(lane == col0, sides[:, ch : ch + 1], block)
            block = jnp.where(lane == col0 + 1, sides[:, 8 + ch : 9 + ch], block)
            out_ref[ch] = block

    @pl.when((lat == 0) | (lat == lats - 1))
    def _():
        row0 = jnp.where(lat == 0, 0, height - 2)
        for which in range(2):
            values = strip(which)
            for ch in range(channels):
                out_ref[ch, pl.ds(row0 + which, 1), :] = values[ch : ch + 1]


def beside(block, axis, step):
    size = lax.axis_size(axis)
    return lax.ppermute(block, axis, [(i, i + step) for i in range(size) if 0 <= i + step < size])


def to_all(block, axis):
    block = jnp.broadcast_to(block[None], (lax.axis_size(axis),) + block.shape)
    return lax.all_to_all(block, axis, 0, 0, tiled=True)


def call(kernel, name, shapes, scratch=(), cost=0, specs=None, count=0, **more):
    return pl.pallas_call(
        functools.partial(kernel, **more) if more else kernel,
        out_shape=shapes,
        in_specs=specs or [VMEM] * count,
        out_specs=jax.tree.map(lambda _: VMEM, shapes),
        scratch_shapes=list(scratch),
        cost_estimate=pl.CostEstimate(flops=cost, bytes_accessed=cost // 4, transcendentals=0),
        name=name,
    )


def inside(array):
    return pltpu.with_memory_space_constraint(array, pltpu.VMEM)


def per_device(
    field, velocity, diffusion, donor_cell, donor_weight, source_tile, source_slot, recv_cell
):
    _, fields, radii, height, breadth = field.shape
    channels = fields * radii
    state = field.reshape(channels, height, breadth)
    speed = velocity.reshape(2 * radii, height, breadth)
    corners = donor_cell.reshape(1, -1)
    weights = donor_weight.reshape(16, -1)
    tiles = source_tile.reshape(1, -1)
    slots = source_slot.reshape(1, -1)
    cells = recv_cell.reshape(1, -1)
    padded = -(-cells.shape[1] // LANES) * LANES
    takers = lax.axis_size(TAKERS)

    def shape(*dims):
        return pltpu.VMEM(dims, F32)

    donated = call(
        donate_kernel,
        "donate",
        shape(8, LANES),
        (pltpu.VMEM((1, LANES), jnp.int32), pltpu.VMEM((16, LANES), F32)),
        4_000_000,
        count=3,
    )(corners, weights, state)
    crossed = lax.ppermute(donated, "panel", [(0, 1), (1, 0)])

    asked = call(
        ask_kernel,
        "ask",
        shape(takers, 8, LANES),
        (pltpu.VMEM((1, padded), jnp.int32), pltpu.VMEM((8, padded), F32)),
        4_000_000,
        count=3,
        height=height,
        breadth=breadth,
    )(tiles, slots, cells)
    asked = lax.all_to_all(asked, TAKERS, 0, 0, tiled=True)

    crossed, state_later = lax.optimization_barrier((crossed, state))
    outer = shape(2 * channels, LANES)
    top, bottom, first, last = call(
        edges_kernel, "edges", [outer] * 4, (), 2_000_000, count=1
    )(state_later)
    above = beside(bottom, "lat", 1)
    below = beside(top, "lat", -1)
    before = beside(last, LON, 1)
    after = beside(first, LON, -1)

    given = to_all(crossed, GIVERS)
    asked, above, below, before, after = lax.optimization_barrier(
        (asked, above, below, before, after)
    )

    taken = call(pick_kernel, "pick", shape(takers, 32, LANES), (), 4_000_000, count=2)(inside(asked), inside(given))
    taken = lax.all_to_all(taken, TAKERS, 0, 0, tiled=True)

    whole = shape(channels, height, breadth)
    advanced = call(
        advance_kernel,
        "advance",
        whole,
        (pltpu.VMEM((channels, height + 16, breadth), F32), pltpu.VMEM((LANES, LANES), F32)),
        6_000_000,
        specs=[SMEM] + [VMEM] * 6,
    )(diffusion, state, speed, *map(inside, (above, below, before, after)))

    stepped = call(
        land_kernel,
        "land",
        jax.ShapeDtypeStruct((channels, height, breadth), F32), (pltpu.VMEM((LANES, LANES), F32),), 4_000_000, count=2
    )(inside(advanced), inside(taken))
    return stepped.reshape(field.shape)


def solution(mesh):
    panels, lats, lons = (mesh.shape[axis] for axis in ("panel", "lat", "lon"))
    grid = Mesh(
        mesh.devices.reshape(panels, lats, lons // 8, 4, 2), ("panel", "lat", "high", "mid", "core")
    )
    placed = (
        P("panel", None, None, "lat", LON),
        P("panel", None, None, "lat", LON),
        P(),
        P("panel", "lat", LON, None),
        P("panel", "lat", LON, None, None),
        P("panel", "lat", LON, None),
        P("panel", "lat", LON, None),
        P("panel", "lat", LON, None),
    )
    return jax.shard_map(
        per_device,
        mesh=grid,
        in_specs=placed,
        out_specs=P("panel", None, None, "lat", LON),
        check_vma=False,
    )
```

time: 82.6 us -> 68 us (0.82)
  the two profiles are of different devices: /device:TPU:8 before, /device:TPU:16 now
where the time goes in v2:
time: 68 us; the launch traced here: 67.5 us
  starting transfers between devices  50.5 us (74%)
  Pallas kernels  8.72 us (13%)
  waiting for transfers between devices  7.51 us (11%)
  local copies, waits for them, and re-layouts  0.69 us (1%)
    all_to_all x1, starting transfers between devices, to_all(): return lax.all_to_all(block, axis, 0, 0, tiled=True)  21.1 us
    ppermute x4, starting transfers between devices, beside(): lax.ppermute(block, axis, [(i, i + step) for i in range(size) if 0 <= i +...  13.2 us
    all_to_all x1, starting transfers between devices, per_device(): taken = lax.all_to_all(taken, TAKERS, 0, 0, tiled=True)  8.39 us
    all_to_all x1, starting transfers between devices, per_device(): asked = lax.all_to_all(asked, TAKERS, 0, 0, tiled=True)  4.3 us
    all_to_all x1, waiting for transfers between devices, per_device(): taken = lax.all_to_all(taken, TAKERS, 0, 0, tiled=True)  4.14 us
    ppermute x1, starting transfers between devices, per_device(): crossed = lax.ppermute(donated, 'panel', [(0, 1), (1, 0)])  3.48 us
    ppermute x1, waiting for transfers between devices, per_device(): crossed = lax.ppermute(donated, 'panel', [(0, 1), (1, 0)])  2.01 us
    pallas_call x1, Pallas kernels, per_device(): call(advance_kernel, 'advance', whole, (pltpu.VMEM((channels, height + 16...  1.98 us
  transfers between devices with their start and end apart: 8, of which 3 were waited for; matrix products, arithmetic and copies ran while one was open for 0% of the time, Pallas kernels for 7%

profile of v2, /device:TPU:16, one launch (start us, length us, event | category | flops | bytes accessed | tf_op | source)
XLA Modules:
  0.0 67.5 jit_solution(7240556822780806765)
XLA Ops:
  0.0 1.7 %ask.1 = f32[8,8,128]{2,1,0:T(8,128)} custom-call(s32[1,508]{1,0:T(1,128)} %bitcast.13, s32[1,508]{1,0:T(1,128)} %bitcast.14, s32[1,508]{1,0:T(1,128)} %bitcast.15), custom_call_target="tpu_custom_call" | custom-call | flops 4000000 | bytes 1000000 | tf_op jit(solution)/shard_map/ask/pallas_call | solution.py:312
  1.7 4.3 %all-to-all-start = ((f32[8,8,128]{2,1,0:T(8,128)}), f32[8,8,128]{2,1,0:T(8,128)S(1)}, u32[]{:S(2)}, u32[]{:S(2)}) async-start(f32[8,8,128]{2,1,0:T(8,128)} %ask.1), calls=%async_computation | async-start | bytes 65536 | tf_op jit(solution)/shard_map/all_to_all | solution.py:322
  6.0 1.4 %donate.1 = f32[8,128]{1,0:T(8,128)S(1)} custom-call(s32[1,118]{1,0:T(1,128)} %bitcast.16, f32[16,118]{1,0:T(8,128)} %bitcast.12, f32[6,128,128]{2,1,0:T(8,128)} %bitcast.8), custom_call_target="tpu_custom_call" | custom-call | flops 4000000 | bytes 1000000 | tf_op jit(solution)/shard_map/donate/pallas_call | solution.py:302
  7.4 3.5 %collective-permute-start = (f32[8,128]{1,0:T(8,128)S(1)}, f32[8,128]{1,0:T(8,128)S(1)}, u32[]{:S(2)}, u32[]{:S(2)}) collective-permute-start(f32[8,128]{1,0:T(8,128)S(1)} %donate.1), channel_id=1, source_target_pairs={{0,384},{384,0},{1,385},{385,1},{2,386},{386,2},{3,387},{387,3},{4... | collective-permute-start | bytes 12296 | tf_op jit(solution)/shard_map/ppermute | solution.py:310
  10.9 2.0 %collective-permute-done = f32[8,128]{1,0:T(8,128)S(1)} collective-permute-done((f32[8,128]{1,0:T(8,128)S(1)}, f32[8,128]{1,0:T(8,128)S(1)}, u32[]{:S(2)}, u32[]{:S(2)}) %collective-permute-start) | collective-permute-done | bytes 4128 | tf_op jit(solution)/shard_map/ppermute | solution.py:310
  12.9 0.0 all-to-all-done.asked_ref
  12.9 0.7 %broadcast_in_dim.2 = f32[48,8,128]{2,1,0:T(8,128)} broadcast(f32[8,128]{1,0:T(8,128)S(1)} %collective-permute-done), dimensions={1,2} | broadcast | bytes 200704 | tf_op jit(solution)/shard_map/broadcast_in_dim | solution.py:264
  13.6 21.1 %all-to-all-start.1 = ((f32[48,8,128]{2,1,0:T(8,128)}), f32[48,8,128]{2,1,0:T(8,128)S(1)}, u32[]{:S(2)}, u32[]{:S(2)}) async-start(f32[48,8,128]{2,1,0:T(8,128)} %broadcast_in_dim.2), calls=%async_computation.1 | async-start | bytes 393216 | tf_op jit(solution)/shard_map/all_to_all | solution.py:265
  34.7 1.3 %edges.1 = (f32[12,128]{1,0:T(8,128)S(1)}, f32[12,128]{1,0:T(8,128)S(1)}, f32[12,128]{1,0:T(8,128)S(1)}, f32[12,128]{1,0:T(8,128)S(1)}) custom-call(f32[6,128,128]{2,1,0:T(8,128)} %bitcast.9), custom_call_target="tpu_custom_call" | custom-call | flops 2000000 | bytes 500000 | tf_op jit(solution)/shard_map/edges/pallas_call | solution.py:326
  36.0 3.4 %collective-permute-start.1 = (f32[12,128]{1,0:T(8,128)S(1)}, f32[12,128]{1,0:T(8,128)S(1)}, u32[]{:S(2)}, u32[]{:S(2)}) collective-permute-start(f32[12,128]{1,0:T(8,128)S(1)} %get-tuple-element.17), channel_id=1, source_target_pairs={{0,32},{32,64},{64,96},{96,128},{128,160},{160,192},{192,224},{224... | collective-permute-start | bytes 18440 | tf_op jit(solution)/shard_map/ppermute | solution.py:260
  39.4 1.3 %collective-permute-start.2 = (f32[12,128]{1,0:T(8,128)S(1)}, f32[12,128]{1,0:T(8,128)S(1)}, u32[]{:S(2)}, u32[]{:S(2)}) collective-permute-start(f32[12,128]{1,0:T(8,128)S(1)} %get-tuple-element.18), channel_id=1, source_target_pairs={{32,0},{64,32},{96,64},{128,96},{160,128},{192,160},{224,192},{256... | collective-permute-start | bytes 18440 | tf_op jit(solution)/shard_map/ppermute | solution.py:260
  40.7 1.9 %collective-permute-start.3 = (f32[12,128]{1,0:T(8,128)S(1)}, f32[12,128]{1,0:T(8,128)S(1)}, u32[]{:S(2)}, u32[]{:S(2)}) collective-permute-start(f32[12,128]{1,0:T(8,128)S(1)} %get-tuple-element.19), channel_id=1, source_target_pairs={{0,1},{1,2},{2,3},{3,4},{4,5},{5,6},{6,7},{7,8},{8,9},{9,10},{10,1... | collective-permute-start | bytes 18440 | tf_op jit(solution)/shard_map/ppermute | solution.py:260
  42.6 6.7 %collective-permute-start.4 = (f32[12,128]{1,0:T(8,128)S(1)}, f32[12,128]{1,0:T(8,128)S(1)}, u32[]{:S(2)}, u32[]{:S(2)}) collective-permute-start(f32[12,128]{1,0:T(8,128)S(1)} %get-tuple-element.20), channel_id=1, source_target_pairs={{1,0},{2,1},{3,2},{4,3},{5,4},{6,5},{7,6},{8,7},{9,8},{10,9},{11,1... | collective-permute-start | bytes 18440 | tf_op jit(solution)/shard_map/ppermute | solution.py:260
  49.3 0.0 collective-permute-done.1.above_ref
  49.3 0.0 collective-permute-done.2.below_ref
  49.3 0.0 collective-permute-done.3.before_ref
  49.3 1.3 %collective-permute-done.4.after_ref = f32[12,128]{1,0:T(8,128)S(1)} collective-permute-done((f32[12,128]{1,0:T(8,128)S(1)}, f32[12,128]{1,0:T(8,128)S(1)}, u32[]{:S(2)}, u32[]{:S(2)}) %collective-permute-start.4) | collective-permute-done | bytes 6176 | tf_op jit(solution)/shard_map/ppermute | solution.py:260
  50.6 0.0 all-to-all-done.1.given_ref
  50.6 1.5 %pick.1 = f32[8,32,128]{2,1,0:T(8,128)} custom-call(f32[8,8,128]{2,1,0:T(8,128)S(1)} %all-to-all-done.asked_ref, f32[48,8,128]{2,1,0:T(8,128)S(1)} %all-to-all-done.1.given_ref), custom_call_target="tpu_custom_call" | custom-call | flops 4000000 | bytes 1000000 | tf_op jit(solution)/shard_map/pick/pallas_call | solution.py:339
  52.2 8.4 %all-to-all-start.2 = ((f32[8,32,128]{2,1,0:T(8,128)}), f32[8,32,128]{2,1,0:T(8,128)S(1)}, u32[]{:S(2)}, u32[]{:S(2)}) async-start(f32[8,32,128]{2,1,0:T(8,128)} %pick.1), calls=%async_computation.2 | async-start | bytes 262144 | tf_op jit(solution)/shard_map/all_to_all | solution.py:340
  60.6 2.0 %advance.1.advanced_ref = f32[6,128,128]{2,1,0:T(8,128)S(1)} custom-call(f32[3]{0:T(128)} %diffusion_ref.1, f32[6,128,128]{2,1,0:T(8,128)} %bitcast.10, f32[4,128,128]{2,1,0:T(8,128)} %bitcast.11, f32[12,128]{1,0:T(8,128)S(1)} %collective-permute-done.1.above_ref, f32[12,128]{1,0:T(8,128)S(1)} %collective-permute-done.2.below_ref, ...), custom_call_target="tpu_custom_call" | custom-call | flops 6000000 | bytes 1500000 | tf_op jit(solution)/shard_map/advance/pallas_call | solution.py:343
  62.6 4.1 %all-to-all-done.2.taken_ref = f32[8,32,128]{2,1,0:T(8,128)S(1)} async-done(((f32[8,32,128]{2,1,0:T(8,128)}), f32[8,32,128]{2,1,0:T(8,128)S(1)}, u32[]{:S(2)}, u32[]{:S(2)}) %all-to-all-start.2) | async-done | bytes 131104 | tf_op jit(solution)/shard_map/all_to_all | solution.py:340
  66.7 0.8 %land.1 = f32[6,128,128]{2,1,0:T(8,128)} custom-call(f32[6,128,128]{2,1,0:T(8,128)S(1)} %advance.1.advanced_ref, f32[8,32,128]{2,1,0:T(8,128)S(1)} %all-to-all-done.2.taken_ref), custom_call_target="tpu_custom_call" | custom-call | flops 4000000 | bytes 1000000 | tf_op jit(solution)/shard_map/land/pallas_call | solution.py:352
Async XLA Ops:
  1.7 11.3 %all-to-all-start = ((f32[8,8,128]{2,1,0:T(8,128)}), f32[8,8,128]{2,1,0:T(8,128)S(1)}, u32[]{:S(2)}, u32[]{:S(2)}) async-start(f32[8,8,128]{2,1,0:T(8,128)} %ask.1), calls=%async_computation | async-start | bytes 65536 | tf_op jit(solution)/shard_map/all_to_all | solution.py:322
  7.4 5.5 %collective-permute-start = (f32[8,128]{1,0:T(8,128)S(1)}, f32[8,128]{1,0:T(8,128)S(1)}, u32[]{:S(2)}, u32[]{:S(2)}) collective-permute-start(f32[8,128]{1,0:T(8,128)S(1)} %donate.1), channel_id=1, source_target_pairs={{0,384},{384,0},{1,385},{385,1},{2,386},{386,2},{3,387},{387,3},{4... | collective-permute-start | bytes 12296 | tf_op jit(solution)/shard_map/ppermute | solution.py:310
  13.6 37.0 %all-to-all-start.1 = ((f32[48,8,128]{2,1,0:T(8,128)}), f32[48,8,128]{2,1,0:T(8,128)S(1)}, u32[]{:S(2)}, u32[]{:S(2)}) async-start(f32[48,8,128]{2,1,0:T(8,128)} %broadcast_in_dim.2), calls=%async_computation.1 | async-start | bytes 393216 | tf_op jit(solution)/shard_map/all_to_all | solution.py:265
  36.0 13.3 %collective-permute-start.1 = (f32[12,128]{1,0:T(8,128)S(1)}, f32[12,128]{1,0:T(8,128)S(1)}, u32[]{:S(2)}, u32[]{:S(2)}) collective-permute-start(f32[12,128]{1,0:T(8,128)S(1)} %get-tuple-element.17), channel_id=1, source_target_pairs={{0,32},{32,64},{64,96},{96,128},{128,160},{160,192},{192,224},{224... | collective-permute-start | bytes 18440 | tf_op jit(solution)/shard_map/ppermute | solution.py:260
  39.4 9.9 %collective-permute-start.2 = (f32[12,128]{1,0:T(8,128)S(1)}, f32[12,128]{1,0:T(8,128)S(1)}, u32[]{:S(2)}, u32[]{:S(2)}) collective-permute-start(f32[12,128]{1,0:T(8,128)S(1)} %get-tuple-element.18), channel_id=1, source_target_pairs={{32,0},{64,32},{96,64},{128,96},{160,128},{192,160},{224,192},{256... | collective-permute-start | bytes 18440 | tf_op jit(solution)/shard_map/ppermute | solution.py:260
  40.7 8.6 %collective-permute-start.3 = (f32[12,128]{1,0:T(8,128)S(1)}, f32[12,128]{1,0:T(8,128)S(1)}, u32[]{:S(2)}, u32[]{:S(2)}) collective-permute-start(f32[12,128]{1,0:T(8,128)S(1)} %get-tuple-element.19), channel_id=1, source_target_pairs={{0,1},{1,2},{2,3},{3,4},{4,5},{5,6},{6,7},{7,8},{8,9},{9,10},{10,1... | collective-permute-start | bytes 18440 | tf_op jit(solution)/shard_map/ppermute | solution.py:260
  42.6 8.0 %collective-permute-start.4 = (f32[12,128]{1,0:T(8,128)S(1)}, f32[12,128]{1,0:T(8,128)S(1)}, u32[]{:S(2)}, u32[]{:S(2)}) collective-permute-start(f32[12,128]{1,0:T(8,128)S(1)} %get-tuple-element.20), channel_id=1, source_target_pairs={{1,0},{2,1},{3,2},{4,3},{5,4},{6,5},{7,6},{8,7},{9,8},{10,9},{11,1... | collective-permute-start | bytes 18440 | tf_op jit(solution)/shard_map/ppermute | solution.py:260
  52.2 14.5 %all-to-all-start.2 = ((f32[8,32,128]{2,1,0:T(8,128)}), f32[8,32,128]{2,1,0:T(8,128)S(1)}, u32[]{:S(2)}, u32[]{:S(2)}) async-start(f32[8,32,128]{2,1,0:T(8,128)} %pick.1), calls=%async_computation.2 | async-start | bytes 262144 | tf_op jit(solution)/shard_map/all_to_all | solution.py:340

commit v3 on v2

--- a/solution.py
+++ b/solution.py
@@ -321,19 +321,19 @@
     )(tiles, slots, cells)
     asked = lax.all_to_all(asked, TAKERS, 0, 0, tiled=True)
 
-    crossed, state_later = lax.optimization_barrier((crossed, state))
     outer = shape(2 * channels, LANES)
     top, bottom, first, last = call(
         edges_kernel, "edges", [outer] * 4, (), 2_000_000, count=1
-    )(state_later)
+    )(state)
+    crossed, top, bottom, first, last = lax.optimization_barrier((crossed, top, bottom, first, last))
+    before = beside(last, LON, 1)
+    after = beside(first, LON, -1)
     above = beside(bottom, "lat", 1)
     below = beside(top, "lat", -1)
-    before = beside(last, LON, 1)
-    after = beside(first, LON, -1)
 
     given = to_all(crossed, GIVERS)
-    asked, above, below, before, after = lax.optimization_barrier(
-        (asked, above, below, before, after)
+    asked, before, after, above, below = lax.optimization_barrier(
+        (asked, before, after, above, below)
     )
 
     taken = call(pick_kernel, "pick", shape(takers, 32, LANES), (), 4_000_000, count=2)(inside(asked), inside(given))

time: 68 us -> 66.7 us (0.981)
  the two profiles are of different devices: /device:TPU:16 before, /device:TPU:1 now
where the time goes in v3:
time: 66.7 us; the launch traced here: 66.1 us
  starting transfers between devices  47.9 us (72%)
  Pallas kernels  8.96 us (13%)
  waiting for transfers between devices  8.48 us (13%)
  local copies, waits for them, and re-layouts  0.69 us (1%)
    all_to_all x1, starting transfers between devices, per_device(): asked = lax.all_to_all(asked, TAKERS, 0, 0, tiled=True)  13.8 us
    all_to_all x1, starting transfers between devices, to_all(): return lax.all_to_all(block, axis, 0, 0, tiled=True)  12.8 us
    ppermute x4, starting transfers between devices, beside(): lax.ppermute(block, axis, [(i, i + step) for i in range(size) if 0 <= i +...  11.5 us
    all_to_all x1, starting transfers between devices, per_device(): taken = lax.all_to_all(taken, TAKERS, 0, 0, tiled=True)  7.94 us
    ppermute x4, waiting for transfers between devices, beside(): lax.ppermute(block, axis, [(i, i + step) for i in range(size) if 0 <= i +...  3.37 us
    all_to_all x1, waiting for transfers between devices, per_device(): taken = lax.all_to_all(taken, TAKERS, 0, 0, tiled=True)  3.28 us
    pallas_call x1, Pallas kernels, per_device(): call(advance_kernel, 'advance', whole, (pltpu.VMEM((channels, height + 16...  1.98 us
    ppermute x1, starting transfers between devices, per_device(): crossed = lax.ppermute(donated, 'panel', [(0, 1), (1, 0)])  1.92 us
  transfers between devices with their start and end apart: 8, of which 4 were waited for; matrix products, arithmetic and copies ran while one was open for 0% of the time, Pallas kernels for 7%

profile of v3, /device:TPU:1, one launch (start us, length us, event | category | flops | bytes accessed | tf_op | source)
XLA Modules:
  0.0 66.1 jit_solution(16839161363059311759)
XLA Ops:
  0.0 1.7 %ask.1 = f32[8,8,128]{2,1,0:T(8,128)} custom-call(s32[1,508]{1,0:T(1,128)} %bitcast.13, s32[1,508]{1,0:T(1,128)} %bitcast.14, s32[1,508]{1,0:T(1,128)} %bitcast.15), custom_call_target="tpu_custom_call" | custom-call | flops 4000000 | bytes 1000000 | tf_op jit(solution)/shard_map/ask/pallas_call | solution.py:312
  1.7 13.8 %all-to-all-start = ((f32[8,8,128]{2,1,0:T(8,128)}), f32[8,8,128]{2,1,0:T(8,128)S(1)}, u32[]{:S(2)}, u32[]{:S(2)}) async-start(f32[8,8,128]{2,1,0:T(8,128)} %ask.1), calls=%async_computation | async-start | bytes 65536 | tf_op jit(solution)/shard_map/all_to_all | solution.py:322
  15.4 1.4 %donate.1 = f32[8,128]{1,0:T(8,128)S(1)} custom-call(s32[1,118]{1,0:T(1,128)} %bitcast.16, f32[16,118]{1,0:T(8,128)} %bitcast.12, f32[6,128,128]{2,1,0:T(8,128)} %bitcast.8), custom_call_target="tpu_custom_call" | custom-call | flops 4000000 | bytes 1000000 | tf_op jit(solution)/shard_map/donate/pallas_call | solution.py:302
  16.9 1.9 %collective-permute-start = (f32[8,128]{1,0:T(8,128)S(1)}, f32[8,128]{1,0:T(8,128)S(1)}, u32[]{:S(2)}, u32[]{:S(2)}) collective-permute-start(f32[8,128]{1,0:T(8,128)S(1)} %donate.1), channel_id=1, source_target_pairs={{0,384},{384,0},{1,385},{385,1},{2,386},{386,2},{3,387},{387,3},{4... | collective-permute-start | bytes 12296 | tf_op jit(solution)/shard_map/ppermute | solution.py:310
  18.8 1.3 %edges.1 = (f32[12,128]{1,0:T(8,128)S(1)}, f32[12,128]{1,0:T(8,128)S(1)}, f32[12,128]{1,0:T(8,128)S(1)}, f32[12,128]{1,0:T(8,128)S(1)}) custom-call(f32[6,128,128]{2,1,0:T(8,128)} %bitcast.9), custom_call_target="tpu_custom_call" | custom-call | flops 2000000 | bytes 500000 | tf_op jit(solution)/shard_map/edges/pallas_call | solution.py:325
  20.1 1.2 %collective-permute-done = f32[8,128]{1,0:T(8,128)S(1)} collective-permute-done((f32[8,128]{1,0:T(8,128)S(1)}, f32[8,128]{1,0:T(8,128)S(1)}, u32[]{:S(2)}, u32[]{:S(2)}) %collective-permute-start) | collective-permute-done | bytes 4128 | tf_op jit(solution)/shard_map/ppermute | solution.py:310
  21.3 0.0 all-to-all-done.asked_ref
  21.3 0.7 %broadcast_in_dim.2 = f32[48,8,128]{2,1,0:T(8,128)} broadcast(f32[8,128]{1,0:T(8,128)S(1)} %collective-permute-done), dimensions={1,2} | broadcast | bytes 200704 | tf_op jit(solution)/shard_map/broadcast_in_dim | solution.py:264
  22.0 12.8 %all-to-all-start.1 = ((f32[48,8,128]{2,1,0:T(8,128)}), f32[48,8,128]{2,1,0:T(8,128)S(1)}, u32[]{:S(2)}, u32[]{:S(2)}) async-start(f32[48,8,128]{2,1,0:T(8,128)} %broadcast_in_dim.2), calls=%async_computation.1 | async-start | bytes 393216 | tf_op jit(solution)/shard_map/all_to_all | solution.py:265
  34.8 5.0 %collective-permute-start.1 = (f32[12,128]{1,0:T(8,128)S(1)}, f32[12,128]{1,0:T(8,128)S(1)}, u32[]{:S(2)}, u32[]{:S(2)}) collective-permute-start(f32[12,128]{1,0:T(8,128)S(1)} %get-tuple-element.23), channel_id=1, source_target_pairs={{0,1},{1,2},{2,3},{3,4},{4,5},{5,6},{6,7},{7,8},{8,9},{9,10},{10,1... | collective-permute-start | bytes 18440 | tf_op jit(solution)/shard_map/ppermute | solution.py:260
  39.8 1.9 %collective-permute-start.2 = (f32[12,128]{1,0:T(8,128)S(1)}, f32[12,128]{1,0:T(8,128)S(1)}, u32[]{:S(2)}, u32[]{:S(2)}) collective-permute-start(f32[12,128]{1,0:T(8,128)S(1)} %get-tuple-element.24), channel_id=1, source_target_pairs={{1,0},{2,1},{3,2},{4,3},{5,4},{6,5},{7,6},{8,7},{9,8},{10,9},{11,1... | collective-permute-start | bytes 18440 | tf_op jit(solution)/shard_map/ppermute | solution.py:260
  41.7 3.3 %collective-permute-start.3 = (f32[12,128]{1,0:T(8,128)S(1)}, f32[12,128]{1,0:T(8,128)S(1)}, u32[]{:S(2)}, u32[]{:S(2)}) collective-permute-start(f32[12,128]{1,0:T(8,128)S(1)} %get-tuple-element.25), channel_id=1, source_target_pairs={{0,32},{32,64},{64,96},{96,128},{128,160},{160,192},{192,224},{224... | collective-permute-start | bytes 18440 | tf_op jit(solution)/shard_map/ppermute | solution.py:260
  45.0 1.3 %collective-permute-start.4 = (f32[12,128]{1,0:T(8,128)S(1)}, f32[12,128]{1,0:T(8,128)S(1)}, u32[]{:S(2)}, u32[]{:S(2)}) collective-permute-start(f32[12,128]{1,0:T(8,128)S(1)} %get-tuple-element.26), channel_id=1, source_target_pairs={{32,0},{64,32},{96,64},{128,96},{160,128},{192,160},{224,192},{256... | collective-permute-start | bytes 18440 | tf_op jit(solution)/shard_map/ppermute | solution.py:260
  46.3 0.0 collective-permute-done.1.before_ref
  46.3 0.0 collective-permute-done.2.after_ref
  46.3 0.0 collective-permute-done.3.above_ref
  46.3 3.4 %collective-permute-done.4.below_ref = f32[12,128]{1,0:T(8,128)S(1)} collective-permute-done((f32[12,128]{1,0:T(8,128)S(1)}, f32[12,128]{1,0:T(8,128)S(1)}, u32[]{:S(2)}, u32[]{:S(2)}) %collective-permute-start.4) | collective-permute-done | bytes 6176 | tf_op jit(solution)/shard_map/ppermute | solution.py:260
  49.7 0.7 %all-to-all-done.1.given_ref = f32[48,8,128]{2,1,0:T(8,128)S(1)} async-done(((f32[48,8,128]{2,1,0:T(8,128)}), f32[48,8,128]{2,1,0:T(8,128)S(1)}, u32[]{:S(2)}, u32[]{:S(2)}) %all-to-all-start.1) | async-done | bytes 196640 | tf_op jit(solution)/shard_map/all_to_all | solution.py:265
  50.4 1.8 %pick.1 = f32[8,32,128]{2,1,0:T(8,128)} custom-call(f32[8,8,128]{2,1,0:T(8,128)S(1)} %all-to-all-done.asked_ref, f32[48,8,128]{2,1,0:T(8,128)S(1)} %all-to-all-done.1.given_ref), custom_call_target="tpu_custom_call" | custom-call | flops 4000000 | bytes 1000000 | tf_op jit(solution)/shard_map/pick/pallas_call | solution.py:339
  52.1 7.9 %all-to-all-start.2 = ((f32[8,32,128]{2,1,0:T(8,128)}), f32[8,32,128]{2,1,0:T(8,128)S(1)}, u32[]{:S(2)}, u32[]{:S(2)}) async-start(f32[8,32,128]{2,1,0:T(8,128)} %pick.1), calls=%async_computation.2 | async-start | bytes 262144 | tf_op jit(solution)/shard_map/all_to_all | solution.py:340
  60.1 2.0 %advance.1.advanced_ref = f32[6,128,128]{2,1,0:T(8,128)S(1)} custom-call(f32[3]{0:T(128)} %diffusion_ref.1, f32[6,128,128]{2,1,0:T(8,128)} %bitcast.10, f32[4,128,128]{2,1,0:T(8,128)} %bitcast.11, f32[12,128]{1,0:T(8,128)S(1)} %collective-permute-done.3.above_ref, f32[12,128]{1,0:T(8,128)S(1)} %collective-permute-done.4.below_ref, ...), custom_call_target="tpu_custom_call" | custom-call | flops 6000000 | bytes 1500000 | tf_op jit(solution)/shard_map/advance/pallas_call | solution.py:343
  62.1 3.3 %all-to-all-done.2.taken_ref = f32[8,32,128]{2,1,0:T(8,128)S(1)} async-done(((f32[8,32,128]{2,1,0:T(8,128)}), f32[8,32,128]{2,1,0:T(8,128)S(1)}, u32[]{:S(2)}, u32[]{:S(2)}) %all-to-all-start.2) | async-done | bytes 131104 | tf_op jit(solution)/shard_map/all_to_all | solution.py:340
  65.4 0.8 %land.1 = f32[6,128,128]{2,1,0:T(8,128)} custom-call(f32[6,128,128]{2,1,0:T(8,128)S(1)} %advance.1.advanced_ref, f32[8,32,128]{2,1,0:T(8,128)S(1)} %all-to-all-done.2.taken_ref), custom_call_target="tpu_custom_call" | custom-call | flops 4000000 | bytes 1000000 | tf_op jit(solution)/shard_map/land/pallas_call | solution.py:352
Async XLA Ops:
  1.7 19.6 %all-to-all-start = ((f32[8,8,128]{2,1,0:T(8,128)}), f32[8,8,128]{2,1,0:T(8,128)S(1)}, u32[]{:S(2)}, u32[]{:S(2)}) async-start(f32[8,8,128]{2,1,0:T(8,128)} %ask.1), calls=%async_computation | async-start | bytes 65536 | tf_op jit(solution)/shard_map/all_to_all | solution.py:322
  16.9 4.4 %collective-permute-start = (f32[8,128]{1,0:T(8,128)S(1)}, f32[8,128]{1,0:T(8,128)S(1)}, u32[]{:S(2)}, u32[]{:S(2)}) collective-permute-start(f32[8,128]{1,0:T(8,128)S(1)} %donate.1), channel_id=1, source_target_pairs={{0,384},{384,0},{1,385},{385,1},{2,386},{386,2},{3,387},{387,3},{4... | collective-permute-start | bytes 12296 | tf_op jit(solution)/shard_map/ppermute | solution.py:310
  22.0 28.4 %all-to-all-start.1 = ((f32[48,8,128]{2,1,0:T(8,128)}), f32[48,8,128]{2,1,0:T(8,128)S(1)}, u32[]{:S(2)}, u32[]{:S(2)}) async-start(f32[48,8,128]{2,1,0:T(8,128)} %broadcast_in_dim.2), calls=%async_computation.1 | async-start | bytes 393216 | tf_op jit(solution)/shard_map/all_to_all | solution.py:265
  34.8 11.5 %collective-permute-start.1 = (f32[12,128]{1,0:T(8,128)S(1)}, f32[12,128]{1,0:T(8,128)S(1)}, u32[]{:S(2)}, u32[]{:S(2)}) collective-permute-start(f32[12,128]{1,0:T(8,128)S(1)} %get-tuple-element.23), channel_id=1, source_target_pairs={{0,1},{1,2},{2,3},{3,4},{4,5},{5,6},{6,7},{7,8},{8,9},{9,10},{10,1... | collective-permute-start | bytes 18440 | tf_op jit(solution)/shard_map/ppermute | solution.py:260
  39.8 6.6 %collective-permute-start.2 = (f32[12,128]{1,0:T(8,128)S(1)}, f32[12,128]{1,0:T(8,128)S(1)}, u32[]{:S(2)}, u32[]{:S(2)}) collective-permute-start(f32[12,128]{1,0:T(8,128)S(1)} %get-tuple-element.24), channel_id=1, source_target_pairs={{1,0},{2,1},{3,2},{4,3},{5,4},{6,5},{7,6},{8,7},{9,8},{10,9},{11,1... | collective-permute-start | bytes 18440 | tf_op jit(solution)/shard_map/ppermute | solution.py:260
  41.7 4.6 %collective-permute-start.3 = (f32[12,128]{1,0:T(8,128)S(1)}, f32[12,128]{1,0:T(8,128)S(1)}, u32[]{:S(2)}, u32[]{:S(2)}) collective-permute-start(f32[12,128]{1,0:T(8,128)S(1)} %get-tuple-element.25), channel_id=1, source_target_pairs={{0,32},{32,64},{64,96},{96,128},{128,160},{160,192},{192,224},{224... | collective-permute-start | bytes 18440 | tf_op jit(solution)/shard_map/ppermute | solution.py:260
  45.0 4.7 %collective-permute-start.4 = (f32[12,128]{1,0:T(8,128)S(1)}, f32[12,128]{1,0:T(8,128)S(1)}, u32[]{:S(2)}, u32[]{:S(2)}) collective-permute-start(f32[12,128]{1,0:T(8,128)S(1)} %get-tuple-element.26), channel_id=1, source_target_pairs={{32,0},{64,32},{96,64},{128,96},{160,128},{192,160},{224,192},{256... | collective-permute-start | bytes 18440 | tf_op jit(solution)/shard_map/ppermute | solution.py:260
  52.1 13.2 %all-to-all-start.2 = ((f32[8,32,128]{2,1,0:T(8,128)}), f32[8,32,128]{2,1,0:T(8,128)S(1)}, u32[]{:S(2)}, u32[]{:S(2)}) async-start(f32[8,32,128]{2,1,0:T(8,128)} %pick.1), calls=%async_computation.2 | async-start | bytes 262144 | tf_op jit(solution)/shard_map/all_to_all | solution.py:340

commit v4 on v3

--- a/solution.py
+++ b/solution.py
@@ -78,15 +78,19 @@
         found = found + lax.dot_general(
             value_ref[:, span].astype(BF16), hit, NT, preferred_element_type=F32
         )
-    for other in range(out_ref.shape[0]):
+    takers = lax.axis_size(TAKERS)
+    base = lax.axis_index("panel") * takers
+    for other in range(takers):
         place = jnp.where(found[1:2] == float(other + 1), found[0:1], -1.0)
         for strip in range(4):
             span = slice(strip * LANES, (strip + 1) * LANES)
-            out_ref[other, strip : strip + 1, :] = place[:, span]
-            out_ref[other, 4 + strip : 5 + strip, :] = found[2:3, span]
+            out_ref[base + other, strip : strip + 1, :] = place[:, span]
+            out_ref[base + other, 4 + strip : 5 + strip, :] = found[2:3, span]
 
 
 def donate_kernel(cell_ref, weight_ref, field_ref, out_ref, corner_ref, padded_ref):
+    takers = lax.axis_size(TAKERS)
+    target = (1 - lax.axis_index("panel")) * takers + lax.axis_index(TAKERS)
     channels, height, breadth = field_ref.shape
     cap = cell_ref.shape[1]
     corner_ref[...] = jnp.zeros(corner_ref.shape, jnp.int32)
@@ -107,13 +111,40 @@
         weights.append(spread)
     picker = jnp.concatenate(columns, axis=1)
     picker = jnp.concatenate([picker, picker], axis=0)
-    out_ref[channels:, :] = jnp.zeros((8 - channels, LANES), F32)
+    out_ref[target, channels:, :] = jnp.zeros((8 - channels, LANES), F32)
     for ch in range(channels):
         along = lax.dot(halves(field_ref[ch]), picker, preferred_element_type=F32)
         total = along[:, :LANES] * weights[0]
         for lateral in range(1, 4):
             total = total + along[:, lateral * LANES : (lateral + 1) * LANES] * weights[lateral]
-        out_ref[ch : ch + 1, :] = jnp.sum(total, axis=0, keepdims=True)
+        out_ref[target, ch : ch + 1, :] = jnp.sum(total, axis=0, keepdims=True)
+
+
+def open_kernel(
+    tile_ref,
+    slot_ref,
+    cell_ref,
+    corner_ref,
+    weight_ref,
+    field_ref,
+    out_ref,
+    key_ref,
+    value_ref,
+    upper_ref,
+    padded_ref,
+):
+    _, height, breadth = field_ref.shape
+    donate_kernel(corner_ref, weight_ref, field_ref, out_ref, upper_ref, padded_ref)
+    ask_kernel(
+        tile_ref, slot_ref, cell_ref, out_ref, key_ref, value_ref, height=height, breadth=breadth
+    )
+
+
+def spread_kernel(arrived_ref, out_ref):
+    takers = lax.axis_size(TAKERS)
+    block = arrived_ref[(1 - lax.axis_index("panel")) * takers + lax.axis_index(TAKERS)]
+    for other in range(out_ref.shape[0]):
+        out_ref[other] = block
 
 
 def edges_kernel(field_ref, top_ref, bottom_ref, first_ref, last_ref):
@@ -136,16 +167,18 @@
 def pick_kernel(asked_ref, given_ref, out_ref):
     lat, lats, lon, lons = position()
     others = out_ref.shape[0]
+    base = lax.axis_index("panel") * others
     donors = given_ref.shape[0]
+    channels = out_ref.shape[1] // 4
     given = halves(given_ref[...].reshape(donors * 8, LANES))
     index = lax.broadcasted_iota(jnp.int32, (LANES, 2 * LANES), 0).astype(F32)
 
     def pick(other, strip):
         place = jnp.concatenate(
-            [asked_ref[other, strip : strip + 1, :], asked_ref[other, strip + 1 : strip + 2, :]], axis=1
+            [asked_ref[base + other, strip : strip + 1, :], asked_ref[base + other, strip + 1 : strip + 2, :]], axis=1
         )
         slot = jnp.concatenate(
-            [asked_ref[other, 4 + strip : 5 + strip, :], asked_ref[other, 5 + strip : 6 + strip, :]], axis=1
+            [asked_ref[base + other, 4 + strip : 5 + strip, :], asked_ref[base + other, 5 + strip : 6 + strip, :]], axis=1
         )
         hit = jnp.where(index == slot, 1.0, 0.0).astype(BF16)
         hit = jnp.concatenate([hit, hit], axis=0)
@@ -153,8 +186,9 @@
         total = jnp.zeros((8, 2 * LANES), F32)
         for donor in range(donors):
             total = total + jnp.where(place == float(donor), values[donor * 8 : donor * 8 + 8], 0.0)
-        out_ref[other, strip * 8 : strip * 8 + 8, :] = total[:, :LANES]
-        out_ref[other, strip * 8 + 8 : strip * 8 + 16, :] = total[:, LANES:]
+        low, middle, high = (step * channels for step in (strip, strip + 1, strip + 2))
+        out_ref[other, low:middle, :] = total[:channels, :LANES]
+        out_ref[other, middle:high, :] = total[:channels, LANES:]
 
     out_ref[...] = jnp.zeros(out_ref.shape, F32)
     mine = lax.axis_index(TAKERS)
@@ -227,16 +261,17 @@
     out_ref[...] = advanced_ref[...]
 
     def strip(which):
-        total = taken_ref[0, which * 8 : which * 8 + 8, :]
+        rows = slice(which * channels, (which + 1) * channels)
+        total = taken_ref[0, rows, :]
         for other in range(1, taken_ref.shape[0]):
-            total = total + taken_ref[other, which * 8 : which * 8 + 8, :]
+            total = total + taken_ref[other, rows, :]
         return total
 
     @pl.when((lon == 0) | (lon == lons - 1))
     def _():
         side_ref[...] = jnp.zeros(side_ref.shape, F32)
-        side_ref[0:8, :] = strip(2)
-        side_ref[8:16, :] = strip(3)
+        side_ref[0:channels, :] = strip(2)
+        side_ref[8 : 8 + channels, :] = strip(3)
         sides = side_ref[...].T
         lane = lax.broadcasted_iota(jnp.int32, (height, breadth), 1)
         col0 = jnp.where(lon == 0, 0, breadth - 2)
@@ -258,11 +293,6 @@
 def beside(block, axis, step):
     size = lax.axis_size(axis)
     return lax.ppermute(block, axis, [(i, i + step) for i in range(size) if 0 <= i + step < size])
-
-
-def to_all(block, axis):
-    block = jnp.broadcast_to(block[None], (lax.axis_size(axis),) + block.shape)
-    return lax.all_to_all(block, axis, 0, 0, tiled=True)
 
 
 def call(kernel, name, shapes, scratch=(), cost=0, specs=None, count=0, **more):
@@ -299,44 +329,40 @@
     def shape(*dims):
         return pltpu.VMEM(dims, F32)
 
-    donated = call(
-        donate_kernel,
-        "donate",
-        shape(8, LANES),
-        (pltpu.VMEM((1, LANES), jnp.int32), pltpu.VMEM((16, LANES), F32)),
-        4_000_000,
-        count=3,
-    )(corners, weights, state)
-    crossed = lax.ppermute(donated, "panel", [(0, 1), (1, 0)])
-
-    asked = call(
-        ask_kernel,
-        "ask",
-        shape(takers, 8, LANES),
-        (pltpu.VMEM((1, padded), jnp.int32), pltpu.VMEM((8, padded), F32)),
-        4_000_000,
-        count=3,
-        height=height,
-        breadth=breadth,
-    )(tiles, slots, cells)
-    asked = lax.all_to_all(asked, TAKERS, 0, 0, tiled=True)
+    opening = call(
+        open_kernel,
+        "open",
+        shape(2 * takers, 8, LANES),
+        (
+            pltpu.VMEM((1, padded), jnp.int32),
+            pltpu.VMEM((8, padded), F32),
+            pltpu.VMEM((1, LANES), jnp.int32),
+            pltpu.VMEM((16, LANES), F32),
+        ),
+        8_000_000,
+        count=6,
+    )(tiles, slots, cells, corners, weights, state)
+    asked = lax.all_to_all(opening, ("panel",) + TAKERS, 0, 0, tiled=True)
 
     outer = shape(2 * channels, LANES)
     top, bottom, first, last = call(
         edges_kernel, "edges", [outer] * 4, (), 2_000_000, count=1
     )(state)
-    crossed, top, bottom, first, last = lax.optimization_barrier((crossed, top, bottom, first, last))
+    asked, top, bottom, first, last = lax.optimization_barrier((asked, top, bottom, first, last))
     before = beside(last, LON, 1)
     after = beside(first, LON, -1)
     above = beside(bottom, "lat", 1)
     below = beside(top, "lat", -1)
 
-    given = to_all(crossed, GIVERS)
+    spread = call(spread_kernel, "spread", shape(lax.axis_size(GIVERS), 8, LANES), (), 100_000, count=1)(
+        inside(asked)
+    )
+    given = lax.all_to_all(spread, GIVERS, 0, 0, tiled=True)
     asked, before, after, above, below = lax.optimization_barrier(
         (asked, before, after, above, below)
     )
 
-    taken = call(pick_kernel, "pick", shape(takers, 32, LANES), (), 4_000_000, count=2)(inside(asked), inside(given))
+    taken = call(pick_kernel, "pick", shape(takers, 4 * channels, LANES), (), 4_000_000, count=2)(inside(asked), inside(given))
     taken = lax.all_to_all(taken, TAKERS, 0, 0, tiled=True)
 
     whole = shape(channels, height, breadth)

time: 66.7 us -> 65.9 us (0.988)
  waiting for transfers between devices: 8.48 us -> 14.8 us
  starting transfers between devices: 47.9 us -> 41.8 us
  local copies, waits for them, and re-layouts: 0.69 us -> 0 us
    all_to_all x2, waiting for transfers between devices: 0.67 us -> 8.47 us  [the longest x1 4.61 us: per_device(): asked = lax.all_to_all(opening, ('panel',) + TAKERS, 0, 0, tiled=True)]
    ppermute x4, starting transfers between devices: 11.5 us -> 9.27 us  [beside(): lax.ppermute(block, axis, [(i, i + step) for i in range(size) if 0 <= i +...]
    all_to_all x1, starting transfers between devices: 7.94 us -> 5.83 us  [per_device(): taken = lax.all_to_all(taken, TAKERS, 0, 0, tiled=True)]
    ppermute x1 -> x0, starting transfers between devices: 1.92 us -> none  [per_device(): crossed = lax.ppermute(donated, 'panel', [(0, 1), (1, 0)])]
    ppermute x1 -> x0, waiting for transfers between devices: 1.16 us -> none  [per_device(): crossed = lax.ppermute(donated, 'panel', [(0, 1), (1, 0)])]
    broadcast_in_dim x1 -> x0, local copies, waits for them, and re-layouts: 0.69 us -> none  [to_all(): block = jnp.broadcast_to(block[None], (lax.axis_size(axis),) + block.shape)]
  transfers between devices with their start and end apart: 8 -> 7, of which waited for: 4 -> 4; matrix products, arithmetic and copies ran while one was open for 0% -> 0% of each run, Pallas kernels for 7% -> 5%
where the time goes in v4:
time: 65.9 us; the launch traced here: 65.5 us
  starting transfers between devices  41.8 us (63%)
  waiting for transfers between devices  14.8 us (22%)
  Pallas kernels  8.77 us (13%)
    all_to_all x1, starting transfers between devices, per_device(): asked = lax.all_to_all(opening, ('panel',) + TAKERS, 0, 0, tiled=True)  13.8 us
    all_to_all x1, starting transfers between devices, per_device(): given = lax.all_to_all(spread, GIVERS, 0, 0, tiled=True)  12.9 us
    ppermute x4, starting transfers between devices, beside(): lax.ppermute(block, axis, [(i, i + step) for i in range(size) if 0 <= i +...  9.27 us
    all_to_all x1, starting transfers between devices, per_device(): taken = lax.all_to_all(taken, TAKERS, 0, 0, tiled=True)  5.83 us
    all_to_all x1, waiting for transfers between devices, per_device(): asked = lax.all_to_all(opening, ('panel',) + TAKERS, 0, 0, tiled=True)  4.61 us
    all_to_all x1, waiting for transfers between devices, per_device(): given = lax.all_to_all(spread, GIVERS, 0, 0, tiled=True)  3.87 us
    ppermute x4, waiting for transfers between devices, beside(): lax.ppermute(block, axis, [(i, i + step) for i in range(size) if 0 <= i +...  3.37 us
    all_to_all x1, waiting for transfers between devices, per_device(): taken = lax.all_to_all(taken, TAKERS, 0, 0, tiled=True)  3.01 us
  transfers between devices with their start and end apart: 7, of which 4 were waited for; matrix products, arithmetic and copies ran while one was open for 0% of the time, Pallas kernels for 5%

profile of v4, /device:TPU:1, one launch (start us, length us, event | category | flops | bytes accessed | tf_op | source)
XLA Modules:
  0.0 65.5 jit_solution(17782527771602769089)
XLA Ops:
  0.0 2.3 %open.1 = f32[16,8,128]{2,1,0:T(8,128)} custom-call(s32[1,508]{1,0:T(1,128)} %bitcast.13, s32[1,508]{1,0:T(1,128)} %bitcast.14, s32[1,508]{1,0:T(1,128)} %bitcast.15, s32[1,118]{1,0:T(1,128)} %bitcast.16, f32[16,118]{1,0:T(8,128)} %bitcast.12, f32[6,128,128]{2,1,0:T(8,128)} %bitcast.8), custom_call_target="tpu_custom_call" | custom-call | flops 8000000 | bytes 2000000 | tf_op jit(solution)/shard_map/open/pallas_call | solution.py:332
  2.3 13.8 %all-to-all-start = ((f32[16,8,128]{2,1,0:T(8,128)}), f32[16,8,128]{2,1,0:T(8,128)S(1)}, u32[]{:S(2)}, u32[]{:S(2)}) async-start(f32[16,8,128]{2,1,0:T(8,128)} %open.1), calls=%async_computation | async-start | bytes 131072 | tf_op jit(solution)/shard_map/all_to_all | solution.py:345
  16.1 1.3 %edges.1 = (f32[12,128]{1,0:T(8,128)S(1)}, f32[12,128]{1,0:T(8,128)S(1)}, f32[12,128]{1,0:T(8,128)S(1)}, f32[12,128]{1,0:T(8,128)S(1)}) custom-call(f32[6,128,128]{2,1,0:T(8,128)} %bitcast.9), custom_call_target="tpu_custom_call" | custom-call | flops 2000000 | bytes 500000 | tf_op jit(solution)/shard_map/edges/pallas_call | solution.py:348
  17.4 4.6 %all-to-all-done.arrived_ref.asked_ref = f32[16,8,128]{2,1,0:T(8,128)S(1)} async-done(((f32[16,8,128]{2,1,0:T(8,128)}), f32[16,8,128]{2,1,0:T(8,128)S(1)}, u32[]{:S(2)}, u32[]{:S(2)}) %all-to-all-start) | async-done | bytes 65568 | tf_op jit(solution)/shard_map/all_to_all | solution.py:345
  22.0 0.7 %spread.1 = f32[48,8,128]{2,1,0:T(8,128)} custom-call(f32[16,8,128]{2,1,0:T(8,128)S(1)} %all-to-all-done.arrived_ref.asked_ref), custom_call_target="tpu_custom_call" | custom-call | flops 100000 | bytes 25000 | tf_op jit(solution)/shard_map/spread/pallas_call | solution.py:357
  22.7 12.9 %all-to-all-start.1 = ((f32[48,8,128]{2,1,0:T(8,128)}), f32[48,8,128]{2,1,0:T(8,128)S(1)}, u32[]{:S(2)}, u32[]{:S(2)}) async-start(f32[48,8,128]{2,1,0:T(8,128)} %spread.1), calls=%async_computation.1 | async-start | bytes 393216 | tf_op jit(solution)/shard_map/all_to_all | solution.py:360
  35.5 2.8 %collective-permute-start = (f32[12,128]{1,0:T(8,128)S(1)}, f32[12,128]{1,0:T(8,128)S(1)}, u32[]{:S(2)}, u32[]{:S(2)}) collective-permute-start(f32[12,128]{1,0:T(8,128)S(1)} %get-tuple-element.24), channel_id=1, source_target_pairs={{0,1},{1,2},{2,3},{3,4},{4,5},{5,6},{6,7},{7,8},{8,9},{9,10},{10,1... | collective-permute-start | bytes 18440 | tf_op jit(solution)/shard_map/ppermute | solution.py:295
  38.3 1.9 %collective-permute-start.1 = (f32[12,128]{1,0:T(8,128)S(1)}, f32[12,128]{1,0:T(8,128)S(1)}, u32[]{:S(2)}, u32[]{:S(2)}) collective-permute-start(f32[12,128]{1,0:T(8,128)S(1)} %get-tuple-element.25), channel_id=1, source_target_pairs={{1,0},{2,1},{3,2},{4,3},{5,4},{6,5},{7,6},{8,7},{9,8},{10,9},{11,1... | collective-permute-start | bytes 18440 | tf_op jit(solution)/shard_map/ppermute | solution.py:295
  40.2 3.3 %collective-permute-start.2 = (f32[12,128]{1,0:T(8,128)S(1)}, f32[12,128]{1,0:T(8,128)S(1)}, u32[]{:S(2)}, u32[]{:S(2)}) collective-permute-start(f32[12,128]{1,0:T(8,128)S(1)} %get-tuple-element.26), channel_id=1, source_target_pairs={{0,32},{32,64},{64,96},{96,128},{128,160},{160,192},{192,224},{224... | collective-permute-start | bytes 18440 | tf_op jit(solution)/shard_map/ppermute | solution.py:295
  43.5 1.3 %collective-permute-start.3 = (f32[12,128]{1,0:T(8,128)S(1)}, f32[12,128]{1,0:T(8,128)S(1)}, u32[]{:S(2)}, u32[]{:S(2)}) collective-permute-start(f32[12,128]{1,0:T(8,128)S(1)} %get-tuple-element.27), channel_id=1, source_target_pairs={{32,0},{64,32},{96,64},{128,96},{160,128},{192,160},{224,192},{256... | collective-permute-start | bytes 18440 | tf_op jit(solution)/shard_map/ppermute | solution.py:295
  44.8 0.0 collective-permute-done.before_ref
  44.9 0.0 collective-permute-done.1.after_ref
  44.9 0.0 collective-permute-done.2.above_ref
  44.9 3.4 %collective-permute-done.3.below_ref = f32[12,128]{1,0:T(8,128)S(1)} collective-permute-done((f32[12,128]{1,0:T(8,128)S(1)}, f32[12,128]{1,0:T(8,128)S(1)}, u32[]{:S(2)}, u32[]{:S(2)}) %collective-permute-start.3) | collective-permute-done | bytes 6176 | tf_op jit(solution)/shard_map/ppermute | solution.py:295
  48.2 3.9 %all-to-all-done.1.given_ref = f32[48,8,128]{2,1,0:T(8,128)S(1)} async-done(((f32[48,8,128]{2,1,0:T(8,128)}), f32[48,8,128]{2,1,0:T(8,128)S(1)}, u32[]{:S(2)}, u32[]{:S(2)}) %all-to-all-start.1) | async-done | bytes 196640 | tf_op jit(solution)/shard_map/all_to_all | solution.py:360
  52.1 1.7 %pick.1 = f32[8,24,128]{2,1,0:T(8,128)} custom-call(f32[16,8,128]{2,1,0:T(8,128)S(1)} %all-to-all-done.arrived_ref.asked_ref, f32[48,8,128]{2,1,0:T(8,128)S(1)} %all-to-all-done.1.given_ref), custom_call_target="tpu_custom_call" | custom-call | flops 4000000 | bytes 1000000 | tf_op jit(solution)/shard_map/pick/pallas_call | solution.py:365
  53.8 5.8 %all-to-all-start.2 = ((f32[8,24,128]{2,1,0:T(8,128)}), f32[8,24,128]{2,1,0:T(8,128)S(1)}, u32[]{:S(2)}, u32[]{:S(2)}) async-start(f32[8,24,128]{2,1,0:T(8,128)} %pick.1), calls=%async_computation.2 | async-start | bytes 196608 | tf_op jit(solution)/shard_map/all_to_all | solution.py:366
  59.7 2.0 %advance.1.advanced_ref = f32[6,128,128]{2,1,0:T(8,128)S(1)} custom-call(f32[3]{0:T(128)} %diffusion_ref.1, f32[6,128,128]{2,1,0:T(8,128)} %bitcast.10, f32[4,128,128]{2,1,0:T(8,128)} %bitcast.11, f32[12,128]{1,0:T(8,128)S(1)} %collective-permute-done.2.above_ref, f32[12,128]{1,0:T(8,128)S(1)} %collective-permute-done.3.below_ref, ...), custom_call_target="tpu_custom_call" | custom-call | flops 6000000 | bytes 1500000 | tf_op jit(solution)/shard_map/advance/pallas_call | solution.py:369
  61.7 3.0 %all-to-all-done.2.taken_ref = f32[8,24,128]{2,1,0:T(8,128)S(1)} async-done(((f32[8,24,128]{2,1,0:T(8,128)}), f32[8,24,128]{2,1,0:T(8,128)S(1)}, u32[]{:S(2)}, u32[]{:S(2)}) %all-to-all-start.2) | async-done | bytes 98336 | tf_op jit(solution)/shard_map/all_to_all | solution.py:366
  64.7 0.8 %land.1 = f32[6,128,128]{2,1,0:T(8,128)} custom-call(f32[6,128,128]{2,1,0:T(8,128)S(1)} %advance.1.advanced_ref, f32[8,24,128]{2,1,0:T(8,128)S(1)} %all-to-all-done.2.taken_ref), custom_call_target="tpu_custom_call" | custom-call | flops 4000000 | bytes 1000000 | tf_op jit(solution)/shard_map/land/pallas_call | solution.py:378
Async XLA Ops:
  2.3 19.7 %all-to-all-start = ((f32[16,8,128]{2,1,0:T(8,128)}), f32[16,8,128]{2,1,0:T(8,128)S(1)}, u32[]{:S(2)}, u32[]{:S(2)}) async-start(f32[16,8,128]{2,1,0:T(8,128)} %open.1), calls=%async_computation | async-start | bytes 131072 | tf_op jit(solution)/shard_map/all_to_all | solution.py:345
  22.7 29.4 %all-to-all-start.1 = ((f32[48,8,128]{2,1,0:T(8,128)}), f32[48,8,128]{2,1,0:T(8,128)S(1)}, u32[]{:S(2)}, u32[]{:S(2)}) async-start(f32[48,8,128]{2,1,0:T(8,128)} %spread.1), calls=%async_computation.1 | async-start | bytes 393216 | tf_op jit(solution)/shard_map/all_to_all | solution.py:360
  35.5 9.3 %collective-permute-start = (f32[12,128]{1,0:T(8,128)S(1)}, f32[12,128]{1,0:T(8,128)S(1)}, u32[]{:S(2)}, u32[]{:S(2)}) collective-permute-start(f32[12,128]{1,0:T(8,128)S(1)} %get-tuple-element.24), channel_id=1, source_target_pairs={{0,1},{1,2},{2,3},{3,4},{4,5},{5,6},{6,7},{7,8},{8,9},{9,10},{10,1... | collective-permute-start | bytes 18440 | tf_op jit(solution)/shard_map/ppermute | solution.py:295
  38.3 6.6 %collective-permute-start.1 = (f32[12,128]{1,0:T(8,128)S(1)}, f32[12,128]{1,0:T(8,128)S(1)}, u32[]{:S(2)}, u32[]{:S(2)}) collective-permute-start(f32[12,128]{1,0:T(8,128)S(1)} %get-tuple-element.25), channel_id=1, source_target_pairs={{1,0},{2,1},{3,2},{4,3},{5,4},{6,5},{7,6},{8,7},{9,8},{10,9},{11,1... | collective-permute-start | bytes 18440 | tf_op jit(solution)/shard_map/ppermute | solution.py:295
  40.2 4.6 %collective-permute-start.2 = (f32[12,128]{1,0:T(8,128)S(1)}, f32[12,128]{1,0:T(8,128)S(1)}, u32[]{:S(2)}, u32[]{:S(2)}) collective-permute-start(f32[12,128]{1,0:T(8,128)S(1)} %get-tuple-element.26), channel_id=1, source_target_pairs={{0,32},{32,64},{64,96},{96,128},{128,160},{160,192},{192,224},{224... | collective-permute-start | bytes 18440 | tf_op jit(solution)/shard_map/ppermute | solution.py:295
  43.5 4.7 %collective-permute-start.3 = (f32[12,128]{1,0:T(8,128)S(1)}, f32[12,128]{1,0:T(8,128)S(1)}, u32[]{:S(2)}, u32[]{:S(2)}) collective-permute-start(f32[12,128]{1,0:T(8,128)S(1)} %get-tuple-element.27), channel_id=1, source_target_pairs={{32,0},{64,32},{96,64},{128,96},{160,128},{192,160},{224,192},{256... | collective-permute-start | bytes 18440 | tf_op jit(solution)/shard_map/ppermute | solution.py:295
  53.8 10.8 %all-to-all-start.2 = ((f32[8,24,128]{2,1,0:T(8,128)}), f32[8,24,128]{2,1,0:T(8,128)S(1)}, u32[]{:S(2)}, u32[]{:S(2)}) async-start(f32[8,24,128]{2,1,0:T(8,128)} %pick.1), calls=%async_computation.2 | async-start | bytes 196608 | tf_op jit(solution)/shard_map/all_to_all | solution.py:366

commit v5 on v4

--- a/solution.py
+++ b/solution.py
@@ -16,7 +16,7 @@
 SMEM = pl.BlockSpec(memory_space=pltpu.SMEM)
 
 
-GIVERS = ("lat", "high")
+GIVERS = ("high", "lat")
 TAKERS = ("mid", "core")
 LON = ("high", "mid", "core")
 

time: 65.9 us -> 65.9 us (level)
  no operation moved by 1% of the time
where the time goes in v5:
time: 65.9 us; the launch traced here: 65.4 us
  starting transfers between devices  42.3 us (64%)
  waiting for transfers between devices  14.2 us (22%)
  Pallas kernels  8.76 us (13%)
    all_to_all x1, starting transfers between devices, per_device(): asked = lax.all_to_all(opening, ('panel',) + TAKERS, 0, 0, tiled=True)  13.8 us
    all_to_all x1, starting transfers between devices, per_device(): given = lax.all_to_all(spread, GIVERS, 0, 0, tiled=True)  12.9 us
    ppermute x4, starting transfers between devices, beside(): lax.ppermute(block, axis, [(i, i + step) for i in range(size) if 0 <= i +...  9.27 us
    all_to_all x1, starting transfers between devices, per_device(): taken = lax.all_to_all(taken, TAKERS, 0, 0, tiled=True)  6.39 us
    all_to_all x1, waiting for transfers between devices, per_device(): asked = lax.all_to_all(opening, ('panel',) + TAKERS, 0, 0, tiled=True)  4.61 us
    ppermute x4, waiting for transfers between devices, beside(): lax.ppermute(block, axis, [(i, i + step) for i in range(size) if 0 <= i +...  3.37 us
    all_to_all x1, waiting for transfers between devices, per_device(): given = lax.all_to_all(spread, GIVERS, 0, 0, tiled=True)  3.25 us
    all_to_all x1, waiting for transfers between devices, per_device(): taken = lax.all_to_all(taken, TAKERS, 0, 0, tiled=True)  3.01 us
  transfers between devices with their start and end apart: 7, of which 4 were waited for; matrix products, arithmetic and copies ran while one was open for 0% of the time, Pallas kernels for 5%

profile of v5, /device:TPU:1, one launch (start us, length us, event | category | flops | bytes accessed | tf_op | source)
XLA Modules:
  0.0 65.4 jit_solution(3722313044743434756)
XLA Ops:
  0.0 2.3 %open.1 = f32[16,8,128]{2,1,0:T(8,128)} custom-call(s32[1,508]{1,0:T(1,128)} %bitcast.13, s32[1,508]{1,0:T(1,128)} %bitcast.14, s32[1,508]{1,0:T(1,128)} %bitcast.15, s32[1,118]{1,0:T(1,128)} %bitcast.16, f32[16,118]{1,0:T(8,128)} %bitcast.12, f32[6,128,128]{2,1,0:T(8,128)} %bitcast.8), custom_call_target="tpu_custom_call" | custom-call | flops 8000000 | bytes 2000000 | tf_op jit(solution)/shard_map/open/pallas_call | solution.py:332
  2.3 13.8 %all-to-all-start = ((f32[16,8,128]{2,1,0:T(8,128)}), f32[16,8,128]{2,1,0:T(8,128)S(1)}, u32[]{:S(2)}, u32[]{:S(2)}) async-start(f32[16,8,128]{2,1,0:T(8,128)} %open.1), calls=%async_computation | async-start | bytes 131072 | tf_op jit(solution)/shard_map/all_to_all | solution.py:345
  16.1 1.3 %edges.1 = (f32[12,128]{1,0:T(8,128)S(1)}, f32[12,128]{1,0:T(8,128)S(1)}, f32[12,128]{1,0:T(8,128)S(1)}, f32[12,128]{1,0:T(8,128)S(1)}) custom-call(f32[6,128,128]{2,1,0:T(8,128)} %bitcast.9), custom_call_target="tpu_custom_call" | custom-call | flops 2000000 | bytes 500000 | tf_op jit(solution)/shard_map/edges/pallas_call | solution.py:348
  17.4 4.6 %all-to-all-done.arrived_ref.asked_ref = f32[16,8,128]{2,1,0:T(8,128)S(1)} async-done(((f32[16,8,128]{2,1,0:T(8,128)}), f32[16,8,128]{2,1,0:T(8,128)S(1)}, u32[]{:S(2)}, u32[]{:S(2)}) %all-to-all-start) | async-done | bytes 65568 | tf_op jit(solution)/shard_map/all_to_all | solution.py:345
  22.0 0.7 %spread.1 = f32[48,8,128]{2,1,0:T(8,128)} custom-call(f32[16,8,128]{2,1,0:T(8,128)S(1)} %all-to-all-done.arrived_ref.asked_ref), custom_call_target="tpu_custom_call" | custom-call | flops 100000 | bytes 25000 | tf_op jit(solution)/shard_map/spread/pallas_call | solution.py:357
  22.7 12.9 %all-to-all-start.1 = ((f32[48,8,128]{2,1,0:T(8,128)}), f32[48,8,128]{2,1,0:T(8,128)S(1)}, u32[]{:S(2)}, u32[]{:S(2)}) async-start(f32[48,8,128]{2,1,0:T(8,128)} %spread.1), calls=%async_computation.1 | async-start | bytes 393216 | tf_op jit(solution)/shard_map/all_to_all | solution.py:360
  35.5 2.8 %collective-permute-start = (f32[12,128]{1,0:T(8,128)S(1)}, f32[12,128]{1,0:T(8,128)S(1)}, u32[]{:S(2)}, u32[]{:S(2)}) collective-permute-start(f32[12,128]{1,0:T(8,128)S(1)} %get-tuple-element.24), channel_id=1, source_target_pairs={{0,1},{1,2},{2,3},{3,4},{4,5},{5,6},{6,7},{7,8},{8,9},{9,10},{10,1... | collective-permute-start | bytes 18440 | tf_op jit(solution)/shard_map/ppermute | solution.py:295
  38.3 1.9 %collective-permute-start.1 = (f32[12,128]{1,0:T(8,128)S(1)}, f32[12,128]{1,0:T(8,128)S(1)}, u32[]{:S(2)}, u32[]{:S(2)}) collective-permute-start(f32[12,128]{1,0:T(8,128)S(1)} %get-tuple-element.25), channel_id=1, source_target_pairs={{1,0},{2,1},{3,2},{4,3},{5,4},{6,5},{7,6},{8,7},{9,8},{10,9},{11,1... | collective-permute-start | bytes 18440 | tf_op jit(solution)/shard_map/ppermute | solution.py:295
  40.2 3.3 %collective-permute-start.2 = (f32[12,128]{1,0:T(8,128)S(1)}, f32[12,128]{1,0:T(8,128)S(1)}, u32[]{:S(2)}, u32[]{:S(2)}) collective-permute-start(f32[12,128]{1,0:T(8,128)S(1)} %get-tuple-element.26), channel_id=1, source_target_pairs={{0,32},{32,64},{64,96},{96,128},{128,160},{160,192},{192,224},{224... | collective-permute-start | bytes 18440 | tf_op jit(solution)/shard_map/ppermute | solution.py:295
  43.5 1.3 %collective-permute-start.3 = (f32[12,128]{1,0:T(8,128)S(1)}, f32[12,128]{1,0:T(8,128)S(1)}, u32[]{:S(2)}, u32[]{:S(2)}) collective-permute-start(f32[12,128]{1,0:T(8,128)S(1)} %get-tuple-element.27), channel_id=1, source_target_pairs={{32,0},{64,32},{96,64},{128,96},{160,128},{192,160},{224,192},{256... | collective-permute-start | bytes 18440 | tf_op jit(solution)/shard_map/ppermute | solution.py:295
  44.8 0.0 collective-permute-done.before_ref
  44.8 0.0 collective-permute-done.1.after_ref
  44.9 0.0 collective-permute-done.2.above_ref
  44.9 3.4 %collective-permute-done.3.below_ref = f32[12,128]{1,0:T(8,128)S(1)} collective-permute-done((f32[12,128]{1,0:T(8,128)S(1)}, f32[12,128]{1,0:T(8,128)S(1)}, u32[]{:S(2)}, u32[]{:S(2)}) %collective-permute-start.3) | collective-permute-done | bytes 6176 | tf_op jit(solution)/shard_map/ppermute | solution.py:295
  48.2 3.3 %all-to-all-done.1.given_ref = f32[48,8,128]{2,1,0:T(8,128)S(1)} async-done(((f32[48,8,128]{2,1,0:T(8,128)}), f32[48,8,128]{2,1,0:T(8,128)S(1)}, u32[]{:S(2)}, u32[]{:S(2)}) %all-to-all-start.1) | async-done | bytes 196640 | tf_op jit(solution)/shard_map/all_to_all | solution.py:360
  51.5 1.8 %pick.1 = f32[8,24,128]{2,1,0:T(8,128)} custom-call(f32[16,8,128]{2,1,0:T(8,128)S(1)} %all-to-all-done.arrived_ref.asked_ref, f32[48,8,128]{2,1,0:T(8,128)S(1)} %all-to-all-done.1.given_ref), custom_call_target="tpu_custom_call" | custom-call | flops 4000000 | bytes 1000000 | tf_op jit(solution)/shard_map/pick/pallas_call | solution.py:365
  53.2 6.4 %all-to-all-start.2 = ((f32[8,24,128]{2,1,0:T(8,128)}), f32[8,24,128]{2,1,0:T(8,128)S(1)}, u32[]{:S(2)}, u32[]{:S(2)}) async-start(f32[8,24,128]{2,1,0:T(8,128)} %pick.1), calls=%async_computation.2 | async-start | bytes 196608 | tf_op jit(solution)/shard_map/all_to_all | solution.py:366
  59.6 2.0 %advance.1.advanced_ref = f32[6,128,128]{2,1,0:T(8,128)S(1)} custom-call(f32[3]{0:T(128)} %diffusion_ref.1, f32[6,128,128]{2,1,0:T(8,128)} %bitcast.10, f32[4,128,128]{2,1,0:T(8,128)} %bitcast.11, f32[12,128]{1,0:T(8,128)S(1)} %collective-permute-done.2.above_ref, f32[12,128]{1,0:T(8,128)S(1)} %collective-permute-done.3.below_ref, ...), custom_call_target="tpu_custom_call" | custom-call | flops 6000000 | bytes 1500000 | tf_op jit(solution)/shard_map/advance/pallas_call | solution.py:369
  61.6 3.0 %all-to-all-done.2.taken_ref = f32[8,24,128]{2,1,0:T(8,128)S(1)} async-done(((f32[8,24,128]{2,1,0:T(8,128)}), f32[8,24,128]{2,1,0:T(8,128)S(1)}, u32[]{:S(2)}, u32[]{:S(2)}) %all-to-all-start.2) | async-done | bytes 98336 | tf_op jit(solution)/shard_map/all_to_all | solution.py:366
  64.6 0.8 %land.1 = f32[6,128,128]{2,1,0:T(8,128)} custom-call(f32[6,128,128]{2,1,0:T(8,128)S(1)} %advance.1.advanced_ref, f32[8,24,128]{2,1,0:T(8,128)S(1)} %all-to-all-done.2.taken_ref), custom_call_target="tpu_custom_call" | custom-call | flops 4000000 | bytes 1000000 | tf_op jit(solution)/shard_map/land/pallas_call | solution.py:378
Async XLA Ops:
  2.3 19.7 %all-to-all-start = ((f32[16,8,128]{2,1,0:T(8,128)}), f32[16,8,128]{2,1,0:T(8,128)S(1)}, u32[]{:S(2)}, u32[]{:S(2)}) async-start(f32[16,8,128]{2,1,0:T(8,128)} %open.1), calls=%async_computation | async-start | bytes 131072 | tf_op jit(solution)/shard_map/all_to_all | solution.py:345
  22.7 28.8 %all-to-all-start.1 = ((f32[48,8,128]{2,1,0:T(8,128)}), f32[48,8,128]{2,1,0:T(8,128)S(1)}, u32[]{:S(2)}, u32[]{:S(2)}) async-start(f32[48,8,128]{2,1,0:T(8,128)} %spread.1), calls=%async_computation.1 | async-start | bytes 393216 | tf_op jit(solution)/shard_map/all_to_all | solution.py:360
  35.5 9.3 %collective-permute-start = (f32[12,128]{1,0:T(8,128)S(1)}, f32[12,128]{1,0:T(8,128)S(1)}, u32[]{:S(2)}, u32[]{:S(2)}) collective-permute-start(f32[12,128]{1,0:T(8,128)S(1)} %get-tuple-element.24), channel_id=1, source_target_pairs={{0,1},{1,2},{2,3},{3,4},{4,5},{5,6},{6,7},{7,8},{8,9},{9,10},{10,1... | collective-permute-start | bytes 18440 | tf_op jit(solution)/shard_map/ppermute | solution.py:295
  38.3 6.6 %collective-permute-start.1 = (f32[12,128]{1,0:T(8,128)S(1)}, f32[12,128]{1,0:T(8,128)S(1)}, u32[]{:S(2)}, u32[]{:S(2)}) collective-permute-start(f32[12,128]{1,0:T(8,128)S(1)} %get-tuple-element.25), channel_id=1, source_target_pairs={{1,0},{2,1},{3,2},{4,3},{5,4},{6,5},{7,6},{8,7},{9,8},{10,9},{11,1... | collective-permute-start | bytes 18440 | tf_op jit(solution)/shard_map/ppermute | solution.py:295
  40.2 4.6 %collective-permute-start.2 = (f32[12,128]{1,0:T(8,128)S(1)}, f32[12,128]{1,0:T(8,128)S(1)}, u32[]{:S(2)}, u32[]{:S(2)}) collective-permute-start(f32[12,128]{1,0:T(8,128)S(1)} %get-tuple-element.26), channel_id=1, source_target_pairs={{0,32},{32,64},{64,96},{96,128},{128,160},{160,192},{192,224},{224... | collective-permute-start | bytes 18440 | tf_op jit(solution)/shard_map/ppermute | solution.py:295
  43.5 4.7 %collective-permute-start.3 = (f32[12,128]{1,0:T(8,128)S(1)}, f32[12,128]{1,0:T(8,128)S(1)}, u32[]{:S(2)}, u32[]{:S(2)}) collective-permute-start(f32[12,128]{1,0:T(8,128)S(1)} %get-tuple-element.27), channel_id=1, source_target_pairs={{32,0},{64,32},{96,64},{128,96},{160,128},{192,160},{224,192},{256... | collective-permute-start | bytes 18440 | tf_op jit(solution)/shard_map/ppermute | solution.py:295
  53.2 11.4 %all-to-all-start.2 = ((f32[8,24,128]{2,1,0:T(8,128)}), f32[8,24,128]{2,1,0:T(8,128)S(1)}, u32[]{:S(2)}, u32[]{:S(2)}) async-start(f32[8,24,128]{2,1,0:T(8,128)} %pick.1), calls=%async_computation.2 | async-start | bytes 196608 | tf_op jit(solution)/shard_map/all_to_all | solution.py:366
